TPU v7x, 32 devices: a whole 2x2x4 slice. The times are simulated.
32 devices in a mesh: doc: 4 (over y, x), seq: 8 (over z, core).
Axes of the slice: x: 2, y: 2, z: 4, core: 2. Of those that a mesh axis runs over, the one named last changes fastest.
Arguments:
- inputs: bfloat16 [16, 1024, 768], P('doc', 'seq'), may hold values from -6 to 6
- question_count: int32 [16], P('doc'), may hold values from 1 to 64, as said below
- question_at: int32 [16, 64], P('doc'), may hold values from 0 to 1023
- local_proj: bfloat16 [2, 768, 2304], replicated, may hold values from -0.21875 to 0.21875
- local_mixer: bfloat16 [2, 768, 768], replicated, may hold values from -1.25 to 1.25
- pooled_proj: bfloat16 [2, 768, 2304], replicated, may hold values from -0.21875 to 0.21875
- pool_taps: float32 [2, 2, 5, 768], replicated, may hold values from -3 to 3
- pooled_mixer: bfloat16 [2, 768, 768], replicated, may hold values from -2.5 to 2.5
- expand_weight: bfloat16 [2, 768, 3072], replicated, may hold values from -0.21875 to 0.21875
- reduce_weight: bfloat16 [2, 3072, 768], replicated, may hold values from -0.109375 to 0.109375
- norm_gain: float32 [2, 3, 768], replicated, may hold values from 0.5 to 1.5
- norm_shift: float32 [2, 3, 768], replicated, may hold values from -1 to 1
- output_grad: bfloat16 [16, 1024, 768], P('doc', 'seq'), may hold values from -6 to 6
Outputs:
- outputs: bfloat16 [16, 1024, 768], P('doc', 'seq')
- input_grad: float32 [16, 1024, 768], P('doc', 'seq')
- local_proj_grad: float32 [2, 768, 2304], P(None, None, 'seq')
- local_mixer_grad: float32 [2, 768, 768], P(None, 'seq')
- pooled_query_grad: float32 [2, 768, 768], P(None, None, 'seq')
- pooled_kv_grad: float32 [2, 768, 1536], P(None, None, 'seq')
- pool_taps_grad: float32 [2, 2, 5, 768], P(None, None, None, 'seq')
- pooled_mixer_grad: float32 [2, 768, 768], P(None, 'seq')
- expand_grad: float32 [2, 768, 3072], P(None, None, 'seq')
- reduce_grad: float32 [2, 3072, 768], P(None, 'seq')
- gain_grad: float32 [2, 3, 768], P(None, None, 'seq')
- shift_grad: float32 [2, 3, 768], P(None, None, 'seq')
Inputs may be any that keep to these rules, and one draw needn't show every extreme that they name: `question_count`: each document has at least one and at most 64 question tokens, and some document has exactly 64. `question_at`: entries of a row past that document's question count are not read; positions may repeat.
All inputs are finite; a program needn't handle non-finite values.
Results may differ from a plain program's by a relative error of at most 0.022.
Values may be sent and summed in bfloat16 or wider, within the bound.
A program may use at most 512 MiB of HBM per device.

v0:
```python
import jax
import jax.numpy as jnp
from jax import lax
from jax.sharding import PartitionSpec as P

HD = 64
LOCAL_WIN = 128
POOL_WIN = 512


EPSILON = 1e-05
MASKED = -1e30


def with_halo(array, sides, width):
    for axis, dim in sides:
        peers, length = (lax.axis_size(axis), array.shape[dim])
        up = [(i, (i + 1) % peers) for i in range(peers - 1)]
        down = [(j, i) for i, j in up]
        last = lax.slice_in_dim(array, length - width, length, axis=dim)
        first = lax.slice_in_dim(array, 0, width, axis=dim)
        before = lax.ppermute(last, axis, up)
        after = lax.ppermute(first, axis, down)
        array = jnp.concatenate([before, array, after], axis=dim)
    return array


def from_behind(value, axis, steps):
    count = lax.axis_size(axis)
    first, last = (max(0, -steps), min(count, count - steps))
    return lax.ppermute(value, axis, [(source, source + steps) for source in range(first, last)])


def layer_norm(summed, gain, shift_bias):
    centre = summed - jnp.mean(summed, -1, keepdims=True)
    spread = jnp.mean(centre * centre, -1, keepdims=True)
    return centre * lax.rsqrt(spread + EPSILON) * gain + shift_bias


def exact_gelu(value):
    return jax.nn.gelu(value, approximate=False)


def mul_plain(left_rows, right_mat):
    return jnp.dot(left_rows, right_mat, preferred_element_type=jnp.float32)


def mul_last(left_rows, right_mat):
    return lax.dot_general(
        left_rows, right_mat, (((1,), (1,)), ((), ())), preferred_element_type=jnp.float32
    )


def mul_first(left_rows, right_rows):
    return lax.dot_general(
        left_rows, right_rows, (((0,), (0,)), ((), ())), preferred_element_type=jnp.float32
    )


def as_rows(array_in):
    return array_in.reshape(-1, array_in.shape[-1])


def masked_scores(queries, key_rows, allowed):
    factor = queries.shape[-1] ** (-0.5)
    scores = (
        jnp.einsum("nqhe,nkhe->nhqk", queries, key_rows, preferred_element_type=jnp.float32)
        * factor
    )
    return (jnp.where(allowed[:, None], scores, MASKED), factor)


def attend(queries, key_rows, value_rows, allowed):
    scores, factor = masked_scores(queries, key_rows, allowed)
    row_top = jnp.max(scores, -1, keepdims=True)
    raised = jnp.exp(scores - row_top)
    row_total = jnp.sum(raised, -1, keepdims=True)
    soft_weights = (raised / row_total).astype(jnp.bfloat16)
    mixed = jnp.einsum(
        "nhqk,nkhe->nqhe", soft_weights, value_rows, preferred_element_type=jnp.float32
    )
    return (mixed, row_top + jnp.log(row_total))


def attend_back(queries, key_rows, value_rows, allowed, log_total, grad_mixed):
    scores, factor = masked_scores(queries, key_rows, allowed)
    soft_full = jnp.exp(scores - log_total)
    soft_weights = soft_full.astype(jnp.bfloat16)
    grad_values = jnp.einsum(
        "nhqk,nqhe->nkhe", soft_weights, grad_mixed, preferred_element_type=jnp.float32
    )
    grad_soft = jnp.einsum(
        "nqhe,nkhe->nhqk", grad_mixed, value_rows, preferred_element_type=jnp.float32
    )
    row_inner = jnp.sum(soft_full * grad_soft, -1, keepdims=True)
    grad_scores = (soft_full * (grad_soft - row_inner)).astype(jnp.bfloat16)
    grad_queries = (
        jnp.einsum("nhqk,nkhe->nqhe", grad_scores, key_rows, preferred_element_type=jnp.float32)
        * factor
    )
    grad_keys = (
        jnp.einsum("nhqk,nqhe->nkhe", grad_scores, queries, preferred_element_type=jnp.float32)
        * factor
    )
    return (grad_queries, grad_keys, grad_values)


def apply_taps(extended, taps):
    pool_rows = (extended.shape[1] - 2) // 4
    total = extended[:, 0 : 4 * pool_rows : 4] * taps[:, 0]
    for tap_at in range(1, 5):
        total = total + extended[:, tap_at : tap_at + 4 * pool_rows : 4] * taps[:, tap_at]
    return total


def taps_back(extended, taps, grad_pool):
    pool_rows = grad_pool.shape[1]
    grad_ext = jnp.zeros(extended.shape, jnp.float32)
    tap_grads = []
    for tap_at in range(5):
        tap_rows = extended[:, tap_at : tap_at + 4 * pool_rows : 4]
        tap_grads.append(jnp.sum(tap_rows * grad_pool, axis=(0, 1)))
        grad_ext = grad_ext.at[:, tap_at : tap_at + 4 * pool_rows : 4].add(
            grad_pool * taps[:, tap_at]
        )
    return (grad_ext, jnp.stack(tap_grads, 1))


def per_device(
    inputs,
    question_count,
    question_at,
    local_proj,
    local_mixer,
    pooled_proj,
    pool_taps,
    pooled_mixer,
    expand_weight,
    reduce_weight,
    norm_gain,
    norm_shift,
    output_grad,
):
    docs_here, tok_here, width = inputs.shape
    layers = local_proj.shape[0]
    heads = width // HD
    half_win = LOCAL_WIN // 2
    seq_count = lax.axis_size("seq")
    seq_at = lax.axis_index("seq")
    length = tok_here * seq_count
    positions = seq_at * tok_here + jnp.arange(tok_here, dtype=jnp.int32)
    slots = jnp.arange(question_at.shape[1], dtype=jnp.int32)
    question = jnp.any(
        (question_at[:, :, None] == positions[None, None, :])
        & (slots[None, :, None] < question_count[:, None, None]),
        axis=1,
    )
    near_cols = seq_at * tok_here - half_win + jnp.arange(tok_here + 2 * half_win, dtype=jnp.int32)
    local_allowed = (
        (jnp.abs(positions[:, None] - near_cols[None, :]) <= half_win)
        & (near_cols[None, :] >= 0)
        & (near_cols[None, :] < length)
    )[None]
    pool_cols = jnp.arange(length // 4, dtype=jnp.int32)
    pool_allowed = (
        jnp.abs(pool_cols[None, None, :] - (positions // 4)[None, :, None]) <= POOL_WIN // 2
    ) | question[:, :, None]
    head_shape = (docs_here, tok_here, heads, HD)
    hidden_now = inputs.astype(jnp.float32)
    saved_all = []
    for layer_at in range(layers):
        in_rows = hidden_now.astype(jnp.bfloat16)
        local_heads = (
            mul_plain(as_rows(in_rows), local_proj[layer_at])
            .astype(jnp.bfloat16)
            .reshape(docs_here, tok_here, 3, heads, HD)
        )
        forward_near_kv = with_halo(local_heads[:, :, 1:], (("seq", 1),), half_win)
        local_result, local_lse = attend(
            local_heads[:, :, 0], forward_near_kv[:, :, 0], forward_near_kv[:, :, 1], local_allowed
        )
        local_mix = local_result.astype(jnp.bfloat16).reshape(docs_here, tok_here, width)
        first_sum = hidden_now + mul_plain(as_rows(local_mix), local_mixer[layer_at]).reshape(
            hidden_now.shape
        )
        first_norm = layer_norm(first_sum, norm_gain[layer_at, 0], norm_shift[layer_at, 0])
        second_in = first_norm.astype(jnp.bfloat16)
        pooled_heads = (
            mul_plain(as_rows(second_in), pooled_proj[layer_at])
            .astype(jnp.bfloat16)
            .reshape(docs_here, tok_here, 3, heads, HD)
        )
        prior_kv = from_behind(pooled_heads[:, tok_here - 2 :, 1:], "seq", 1)
        extended = jnp.concatenate([prior_kv, pooled_heads[:, :, 1:]], 1).astype(jnp.float32)
        forward_taps = pool_taps[layer_at].reshape(2, 5, heads, HD)
        pooled = apply_taps(extended, forward_taps).astype(jnp.bfloat16)
        forward_all_pooled = lax.all_gather(pooled, "seq", axis=1, tiled=True)
        pooled_result, pooled_lse = attend(
            pooled_heads[:, :, 0],
            forward_all_pooled[:, :, 0],
            forward_all_pooled[:, :, 1],
            pool_allowed,
        )
        pooled_mix = pooled_result.astype(jnp.bfloat16).reshape(docs_here, tok_here, width)
        second_sum = first_norm + mul_plain(as_rows(pooled_mix), pooled_mixer[layer_at]).reshape(
            hidden_now.shape
        )
        second_norm = layer_norm(second_sum, norm_gain[layer_at, 1], norm_shift[layer_at, 1])
        ffn_in = second_norm.astype(jnp.bfloat16)
        up_proj = mul_plain(as_rows(ffn_in), expand_weight[layer_at])
        activated = exact_gelu(up_proj).astype(jnp.bfloat16)
        third_sum = second_norm + mul_plain(activated, reduce_weight[layer_at]).reshape(
            hidden_now.shape
        )
        result = layer_norm(third_sum, norm_gain[layer_at, 2], norm_shift[layer_at, 2])
        forward_saved = {
            "in_rows": in_rows,
            "local_heads": local_heads,
            "near_kv": forward_near_kv,
            "local_lse": local_lse,
            "local_mix": local_mix,
            "first_sum": first_sum,
            "second_in": second_in,
            "pooled_heads": pooled_heads,
            "extended": extended,
            "saved_pool": forward_all_pooled,
            "pooled_lse": pooled_lse,
            "pooled_mix": pooled_mix,
            "second_sum": second_sum,
            "ffn_in": ffn_in,
            "up_proj": up_proj,
            "activated": activated,
            "third_sum": third_sum,
        }
        hidden_now = result
        saved_all.append(forward_saved)
    outputs = hidden_now.astype(jnp.bfloat16)
    grad_now = output_grad.astype(jnp.float32)
    grads_list = [None] * layers
    for layer_at in reversed(range(layers)):
        backward_saved = saved_all[layer_at]
        gain_row = norm_gain[layer_at]
        bias_row = norm_shift[layer_at]
        taps = pool_taps[layer_at].reshape(2, 5, heads, HD)
        unused_third, pull_third = jax.vjp(
            layer_norm, backward_saved["third_sum"], gain_row[2], bias_row[2]
        )
        grad_third, gain_third, bias_third = pull_third(grad_now)
        grad_down_in = as_rows(grad_third.astype(jnp.bfloat16))
        down_grad = mul_first(backward_saved["activated"], grad_down_in)
        grad_act = mul_last(grad_down_in, reduce_weight[layer_at])
        unused_gelu, pull_gelu = jax.vjp(exact_gelu, backward_saved["up_proj"])
        grad_up = pull_gelu(grad_act)[0].astype(jnp.bfloat16)
        up_grad = mul_first(as_rows(backward_saved["ffn_in"]), grad_up)
        grad_second = grad_third + mul_last(grad_up, expand_weight[layer_at]).reshape(
            grad_now.shape
        )
        unused_second, pull_second = jax.vjp(
            layer_norm, backward_saved["second_sum"], gain_row[1], bias_row[1]
        )
        grad_mid, gain_second, bias_second = pull_second(grad_second)
        grad_pool_mix = as_rows(grad_mid.astype(jnp.bfloat16))
        out2_grad = mul_first(as_rows(backward_saved["pooled_mix"]), grad_pool_mix)
        grad_pool_out = (
            mul_last(grad_pool_mix, pooled_mixer[layer_at]).astype(jnp.bfloat16).reshape(head_shape)
        )
        all_pooled = backward_saved["saved_pool"]
        grad_pool_query, grad_pool_key, grad_pool_value = attend_back(
            backward_saved["pooled_heads"][:, :, 0],
            all_pooled[:, :, 0],
            all_pooled[:, :, 1],
            pool_allowed,
            backward_saved["pooled_lse"],
            grad_pool_out,
        )
        own_key = lax.psum_scatter(
            grad_pool_key.astype(jnp.bfloat16), "seq", scatter_dimension=1, tiled=True
        ).astype(jnp.float32)
        own_value = lax.psum_scatter(
            grad_pool_value.astype(jnp.bfloat16), "seq", scatter_dimension=1, tiled=True
        ).astype(jnp.float32)
        grad_ext, taps_grad = taps_back(
            backward_saved["extended"], taps, jnp.stack([own_key, own_value], 2)
        )
        from_next = from_behind(grad_ext[:, :2].astype(jnp.bfloat16), "seq", -1).astype(jnp.float32)
        grad_kv_second = grad_ext[:, 2:].at[:, tok_here - 2 :].add(from_next)
        grad_heads_two = (
            jnp.concatenate([grad_pool_query[:, :, None], grad_kv_second], 2)
            .astype(jnp.bfloat16)
            .reshape(-1, 3 * width)
        )
        proj2_grad = mul_first(as_rows(backward_saved["second_in"]), grad_heads_two)
        grad_first = grad_mid + mul_last(grad_heads_two, pooled_proj[layer_at]).reshape(
            grad_now.shape
        )
        unused_first, pull_first = jax.vjp(
            layer_norm, backward_saved["first_sum"], gain_row[0], bias_row[0]
        )
        grad_low, gain_first, bias_first = pull_first(grad_first)
        grad_local_mix = as_rows(grad_low.astype(jnp.bfloat16))
        out1_grad = mul_first(as_rows(backward_saved["local_mix"]), grad_local_mix)
        grad_local_out = (
            mul_last(grad_local_mix, local_mixer[layer_at]).astype(jnp.bfloat16).reshape(head_shape)
        )
        near_kv = backward_saved["near_kv"]
        grad_local_query, grad_near_key, grad_near_value = attend_back(
            backward_saved["local_heads"][:, :, 0],
            near_kv[:, :, 0],
            near_kv[:, :, 1],
            local_allowed,
            backward_saved["local_lse"],
            grad_local_out,
        )
        grad_near = jnp.stack([grad_near_key, grad_near_value], 2)
        rim_rows = jnp.concatenate(
            [grad_near[:, :half_win], grad_near[:, tok_here + half_win :]], 1
        )
        came_back = with_halo(rim_rows.astype(jnp.bfloat16), (("seq", 1),), half_win).astype(
            rim_rows.dtype
        )
        grad_kv_first = grad_near[:, half_win : half_win + tok_here]
        grad_kv_first = grad_kv_first.at[:, :half_win].add(came_back[:, :half_win])
        grad_kv_first = grad_kv_first.at[:, tok_here - half_win :].add(came_back[:, 3 * half_win :])
        grad_heads_one = (
            jnp.concatenate([grad_local_query[:, :, None], grad_kv_first], 2)
            .astype(jnp.bfloat16)
            .reshape(-1, 3 * width)
        )
        proj1_grad = mul_first(as_rows(backward_saved["in_rows"]), grad_heads_one)
        grad_bottom = grad_low + mul_last(grad_heads_one, local_proj[layer_at]).reshape(
            grad_now.shape
        )
        layer_grads = (
            proj1_grad,
            out1_grad,
            proj2_grad[:, :width],
            proj2_grad[:, width:],
            taps_grad.reshape(2, 5, width),
            out2_grad,
            up_grad,
            down_grad,
            jnp.stack([gain_first, gain_second, gain_third]),
            jnp.stack([bias_first, bias_second, bias_third]),
        )
        grad_now, layer_grads = (grad_bottom, layer_grads)
        grads_list[layer_at] = layer_grads
    stacked = [jnp.stack([layer_set[member] for layer_set in grads_list]) for member in range(10)]
    shards_all = (
        lax.psum_scatter(
            stacked[0].astype(jnp.bfloat16), "seq", scatter_dimension=2, tiled=True
        ).astype(jnp.float32),
        lax.psum_scatter(
            stacked[1].astype(jnp.bfloat16), "seq", scatter_dimension=1, tiled=True
        ).astype(jnp.float32),
        lax.psum_scatter(
            stacked[2].astype(jnp.bfloat16), "seq", scatter_dimension=2, tiled=True
        ).astype(jnp.float32),
        lax.psum_scatter(
            stacked[3].astype(jnp.bfloat16), "seq", scatter_dimension=2, tiled=True
        ).astype(jnp.float32),
        lax.psum_scatter(
            stacked[4].astype(jnp.bfloat16), "seq", scatter_dimension=3, tiled=True
        ).astype(jnp.float32),
        lax.psum_scatter(
            stacked[5].astype(jnp.bfloat16), "seq", scatter_dimension=1, tiled=True
        ).astype(jnp.float32),
        lax.psum_scatter(
            stacked[6].astype(jnp.bfloat16), "seq", scatter_dimension=2, tiled=True
        ).astype(jnp.float32),
        lax.psum_scatter(
            stacked[7].astype(jnp.bfloat16), "seq", scatter_dimension=1, tiled=True
        ).astype(jnp.float32),
        lax.psum_scatter(
            stacked[8].astype(jnp.bfloat16), "seq", scatter_dimension=2, tiled=True
        ).astype(jnp.float32),
        lax.psum_scatter(
            stacked[9].astype(jnp.bfloat16), "seq", scatter_dimension=2, tiled=True
        ).astype(jnp.float32),
    )
    stacked = (
        lax.psum(shards_all[0].astype(jnp.bfloat16), "doc").astype(jnp.float32),
        lax.psum(shards_all[1].astype(jnp.bfloat16), "doc").astype(jnp.float32),
        lax.psum(shards_all[2].astype(jnp.bfloat16), "doc").astype(jnp.float32),
        lax.psum(shards_all[3].astype(jnp.bfloat16), "doc").astype(jnp.float32),
        lax.psum(shards_all[4].astype(jnp.bfloat16), "doc").astype(jnp.float32),
        lax.psum(shards_all[5].astype(jnp.bfloat16), "doc").astype(jnp.float32),
        lax.psum(shards_all[6].astype(jnp.bfloat16), "doc").astype(jnp.float32),
        lax.psum(shards_all[7].astype(jnp.bfloat16), "doc").astype(jnp.float32),
        lax.psum(shards_all[8].astype(jnp.bfloat16), "doc").astype(jnp.float32),
        lax.psum(shards_all[9].astype(jnp.bfloat16), "doc").astype(jnp.float32),
    )
    return (
        outputs,
        grad_now,
        stacked[0],
        stacked[1],
        stacked[2],
        stacked[3],
        stacked[4],
        stacked[5],
        stacked[6],
        stacked[7],
        stacked[8],
        stacked[9],
    )


def solution(mesh):
    return jax.shard_map(
        per_device,
        mesh=mesh,
        in_specs=(
            P("doc", "seq", None),
            P("doc"),
            P("doc", None),
            P(),
            P(),
            P(),
            P(),
            P(),
            P(),
            P(),
            P(),
            P(),
            P("doc", "seq", None),
        ),
        out_specs=(
            P("doc", "seq", None),
            P("doc", "seq", None),
            P(None, None, "seq"),
            P(None, "seq", None),
            P(None, None, "seq"),
            P(None, None, "seq"),
            P(None, None, None, "seq"),
            P(None, "seq", None),
            P(None, None, "seq"),
            P(None, "seq", None),
            P(None, None, "seq"),
            P(None, None, "seq"),
        ),
        check_vma=False,
    )
```

profile of v0, /device:TPU:0, one launch (start us, length us, event | category | flops | bytes accessed | tf_op | source)
XLA Modules:
  0.0 2497.1 jit_solution(14216451600433754509)
XLA Ops:
  66.9 18.9 collective-permute-start.2
  95.4 52.9 %slice.563 = f32[4,32,2,12,64]{1,0,4,3,2:T(4,128)} slice(f32[4,130,2,12,64]{1,0,4,3,2:T(4,128)} %maximum_convert_fusion), slice={[0:4:1], [0:128:4], [0:2:1], [0:12:1], [0:64:1]} | slice | bytes 1572864 | tf_op jit(solution)/shard_map/slice | solution.py:110
  148.3 53.5 %slice.566 = f32[4,32,2,12,64]{1,0,4,3,2:T(4,128)} slice(f32[4,130,2,12,64]{1,0,4,3,2:T(4,128)} %maximum_convert_fusion), slice={[0:4:1], [1:129:4], [0:2:1], [0:12:1], [0:64:1]} | slice | bytes 1572864 | tf_op jit(solution)/shard_map/slice | solution.py:112
  201.9 53.5 %slice.568 = f32[4,32,2,12,64]{1,0,4,3,2:T(4,128)} slice(f32[4,130,2,12,64]{1,0,4,3,2:T(4,128)} %maximum_convert_fusion), slice={[0:4:1], [2:130:4], [0:2:1], [0:12:1], [0:64:1]} | slice | bytes 1572864 | tf_op jit(solution)/shard_map/slice | solution.py:112
  255.4 53.5 %slice.570 = f32[4,32,2,12,64]{1,0,4,3,2:T(4,128)} slice(f32[4,130,2,12,64]{1,0,4,3,2:T(4,128)} %maximum_convert_fusion), slice={[0:4:1], [3:130:4], [0:2:1], [0:12:1], [0:64:1]} | slice | bytes 1572864 | tf_op jit(solution)/shard_map/slice | solution.py:112
  308.9 53.6 %slice.572 = f32[4,32,2,12,64]{1,0,4,3,2:T(4,128)} slice(f32[4,130,2,12,64]{1,0,4,3,2:T(4,128)} %maximum_convert_fusion), slice={[0:4:1], [4:130:4], [0:2:1], [0:12:1], [0:64:1]} | slice | bytes 1572864 | tf_op jit(solution)/shard_map/slice | solution.py:112
  380.0 64.0 %all-gather.3.cloned.1.call-done = bf16[4,256,2,12,64]{4,0,3,2,1:T(4,128)(2,1)} async-done(((bf16[4,32,2,12,64]{4,0,3,2,1:T(4,128)(2,1)}), bf16[4,256,2,12,64]{4,0,3,2,1:T(4,128)(2,1)}) %all-gather.3.cloned.1.call-update) | async-done | bytes 3145744 | tf_op jit(solution)/shard_map/all_gather | solution.py:197
  473.4 18.7 multiply_convert_fusion.5
  580.8 52.9 %slice.597 = f32[4,32,2,12,64]{1,0,4,3,2:T(4,128)} slice(f32[4,130,2,12,64]{1,0,4,3,2:T(4,128)} %maximum_convert_fusion.1), slice={[0:4:1], [0:128:4], [0:2:1], [0:12:1], [0:64:1]} | slice | bytes 1572864 | tf_op jit(solution)/shard_map/slice | solution.py:110
  633.7 53.5 %slice.600 = f32[4,32,2,12,64]{1,0,4,3,2:T(4,128)} slice(f32[4,130,2,12,64]{1,0,4,3,2:T(4,128)} %maximum_convert_fusion.1), slice={[0:4:1], [1:129:4], [0:2:1], [0:12:1], [0:64:1]} | slice | bytes 1572864 | tf_op jit(solution)/shard_map/slice | solution.py:112
  687.3 53.5 %slice.602 = f32[4,32,2,12,64]{1,0,4,3,2:T(4,128)} slice(f32[4,130,2,12,64]{1,0,4,3,2:T(4,128)} %maximum_convert_fusion.1), slice={[0:4:1], [2:130:4], [0:2:1], [0:12:1], [0:64:1]} | slice | bytes 1572864 | tf_op jit(solution)/shard_map/slice | solution.py:112
  740.8 53.5 %slice.604 = f32[4,32,2,12,64]{1,0,4,3,2:T(4,128)} slice(f32[4,130,2,12,64]{1,0,4,3,2:T(4,128)} %maximum_convert_fusion.1), slice={[0:4:1], [3:130:4], [0:2:1], [0:12:1], [0:64:1]} | slice | bytes 1572864 | tf_op jit(solution)/shard_map/slice | solution.py:112
  794.3 53.6 %slice.606 = f32[4,32,2,12,64]{1,0,4,3,2:T(4,128)} slice(f32[4,130,2,12,64]{1,0,4,3,2:T(4,128)} %maximum_convert_fusion.1), slice={[0:4:1], [4:130:4], [0:2:1], [0:12:1], [0:64:1]} | slice | bytes 1572864 | tf_op jit(solution)/shard_map/slice | solution.py:112
  865.0 63.1 %all-gather.5.cloned.1.call-done = bf16[4,256,2,12,64]{4,0,3,2,1:T(4,128)(2,1)} async-done(((bf16[4,32,2,12,64]{4,0,3,2,1:T(4,128)(2,1)}), bf16[4,256,2,12,64]{4,0,3,2,1:T(4,128)(2,1)}) %all-gather.5.cloned.1.call-update) | async-done | bytes 3145744 | tf_op jit(solution)/shard_map/all_gather | solution.py:197
  1030.6 129.9 %all-reduce.20.cloned.1.call-done = (bf16[4,256,12,64]{3,0,2,1:T(4,128)(2,1)}, bf16[4,256,12,64]{3,0,2,1:T(4,128)(2,1)}) async-done(((bf16[4,256,12,64]{3,0,2,1:T(4,128)(2,1)}, bf16[4,256,12,64]{3,0,2,1:T(4,128)(2,1)}), (bf16[4,256,12,64]{3,0,2,1:T(4,128)(2,1)}, bf16[4,256,12,64]{3,0,2,1:T(4,128)(2,1)})) %all-reduce.20.cloned.1.call-update) | async-done | bytes 3145744
  1165.7 27.8 %fusion.87 = (bf16[2,12,64]{2,1,0:T(8,128)(2,1)}, bf16[2,12,64]{2,1,0:T(8,128)(2,1)}, bf16[2,12,64]{2,1,0:T(8,128)(2,1)}, bf16[2,12,64]{2,1,0:T(8,128)(2,1)}, bf...) fusion(f32[4,32,2,12,64]{1,0,4,3,2:T(4,128)} %slice.606, ...), kind=kLoop, calls=%fused_computation.187 | loop fusion | flops 3531264 | bytes 7511040 | tf_op jit(solution)/shard_map/reduce_sum | solution.py:122
  1320.5 30.5 %scatter-add.106 = f32[4,128,2,12,64]{1,4,3,0,2:T(8,128)S(1)} dynamic-update-slice(f32[4,128,2,12,64]{1,4,3,0,2:T(8,128)S(1)} %fusion.75, f32[4,64,2,12,64]{1,4,3,0,2:T(8,128)} %fusion.77, s32[]{:T(128)} %constant.235.clone.1, s32[]{:T(128)} %constant.235.clone.1, s32[]{:T(128)} %constant.235.clone.1, s32[]{:T(128)} %constant.235.clone.1, s32[]{:T(128)} %constant.235.clone.1) | dynamic-update-slice | bytes 3145732 | tf_op jit(solution)/shard_map/scatter-add | solution.py:322
  1356.3 39.3 %scatter-add.107 = f32[4,128,2,12,64]{1,4,3,0,2:T(8,128)S(1)} dynamic-update-slice(f32[4,128,2,12,64]{1,4,3,0,2:T(8,128)S(1)} %scatter-add.106, f32[4,64,2,12,64]{1,4,3,0,2:T(8,128)} %slice_add_fusion.1, s32[]{:T(128)} %constant.235.clone.1, s32[]{:T(128)} %constant.234.clone.1, s32[]{:T(128)} %constant.235.clone.1, s32[]{:T(128)} %constant.235.clone.1, s32[]{:T(128)} %constant.235.clone.1) | dynamic-update-slice | bytes 3145732 | tf_op jit(solution)/shard_map/scatter-add | solution.py:323
  1460.0 140.1 %all-reduce.18.cloned.1.call-done = (bf16[4,256,12,64]{3,0,2,1:T(4,128)(2,1)}, bf16[4,256,12,64]{3,0,2,1:T(4,128)(2,1)}) async-done(((bf16[4,256,12,64]{3,0,2,1:T(4,128)(2,1)}, bf16[4,256,12,64]{3,0,2,1:T(4,128)(2,1)}), (bf16[4,256,12,64]{3,0,2,1:T(4,128)(2,1)}, bf16[4,256,12,64]{3,0,2,1:T(4,128)(2,1)})) %all-reduce.18.cloned.1.call-update) | async-done | bytes 3145744
  1605.0 27.8 %fusion.97 = (bf16[2,12,64]{2,1,0:T(8,128)(2,1)}, bf16[2,12,64]{2,1,0:T(8,128)(2,1)}, bf16[2,12,64]{2,1,0:T(8,128)(2,1)}, bf16[2,12,64]{2,1,0:T(8,128)(2,1)}, bf...) fusion(f32[4,32,2,12,64]{1,0,4,3,2:T(4,128)} %slice.572, ...), kind=kLoop, calls=%fused_computation.197 | loop fusion | flops 3531264 | bytes 7511040 | tf_op jit(solution)/shard_map/reduce_sum | solution.py:122
  1763.5 23.9 copy.309
  1868.0 30.5 %scatter-add.114 = f32[4,128,2,12,64]{1,4,3,0,2:T(8,128)S(1)} dynamic-update-slice(f32[4,128,2,12,64]{1,4,3,0,2:T(8,128)S(1)} %fusion.72, f32[4,64,2,12,64]{1,4,3,0,2:T(8,128)} %fusion.74, s32[]{:T(128)} %constant.235.clone.1, s32[]{:T(128)} %constant.235.clone.1, s32[]{:T(128)} %constant.235.clone.1, s32[]{:T(128)} %constant.235.clone.1, s32[]{:T(128)} %constant.235.clone.1) | dynamic-update-slice | bytes 3145732 | tf_op jit(solution)/shard_map/scatter-add | solution.py:322
  1903.8 39.3 %scatter-add.115 = f32[4,128,2,12,64]{1,4,3,0,2:T(8,128)S(1)} dynamic-update-slice(f32[4,128,2,12,64]{1,4,3,0,2:T(8,128)S(1)} %scatter-add.114, f32[4,64,2,12,64]{1,4,3,0,2:T(8,128)} %slice_add_fusion, s32[]{:T(128)} %constant.235.clone.1, s32[]{:T(128)} %constant.234.clone.1, s32[]{:T(128)} %constant.235.clone.1, s32[]{:T(128)} %constant.235.clone.1, s32[]{:T(128)} %constant.235.clone.1) | dynamic-update-slice | bytes 3145732 | tf_op jit(solution)/shard_map/scatter-add | solution.py:323
  1991.8 22.9 reduce-scatter.27.cloned.1.call-done
  2020.8 30.6 %reduce-scatter.21.cloned.1.call-done = bf16[2,96,768]{2,1,0:T(8,128)(2,1)} async-done(((bf16[2,768,768]{2,1,0:T(8,128)(2,1)}), bf16[2,96,768]{2,1,0:T(8,128)(2,1)}) %reduce-scatter.21.cloned.1.call-update) | async-done | bytes 294928 | tf_op jit(solution)/shard_map/reduce_scatter | solution.py:364
  2051.5 38.5 %reduce-scatter.19.cloned.1.call-done = bf16[2,96,768]{2,1,0:T(8,128)(2,1)} async-done(((bf16[2,768,768]{2,1,0:T(8,128)(2,1)}), bf16[2,96,768]{2,1,0:T(8,128)(2,1)}) %reduce-scatter.19.cloned.1.call-update) | async-done | bytes 294928 | tf_op jit(solution)/shard_map/reduce_scatter | solution.py:352
  2090.0 78.7 %reduce-scatter.17.cloned.1.call-done = bf16[2,768,288]{1,2,0:T(8,128)(2,1)} async-done(((bf16[2,768,2304]{1,2,0:T(8,128)(2,1)}), bf16[2,768,288]{1,2,0:T(8,128)(2,1)}) %reduce-scatter.17.cloned.1.call-update) | async-done | bytes 884752 | tf_op jit(solution)/shard_map/reduce_scatter | solution.py:349
  2168.7 100.0 %reduce-scatter.23.cloned.1.call-done = bf16[2,384,768]{2,1,0:T(8,128)(2,1)} async-done(((bf16[2,3072,768]{2,1,0:T(8,128)(2,1)}), bf16[2,384,768]{2,1,0:T(8,128)(2,1)}) %reduce-scatter.23.cloned.1.call-update) | async-done | bytes 1179664 | tf_op jit(solution)/shard_map/reduce_scatter | solution.py:370
  2268.8 31.5 %reduce-scatter.31.cloned.1.call-done = bf16[96,6]{1,0:T(8,128)(2,1)} async-done(((bf16[768,6]{1,0:T(8,128)(2,1)}), bf16[96,6]{1,0:T(8,128)(2,1)}) %reduce-scatter.31.cloned.1.call-update) | async-done | bytes 1168
  2301.2 30.3 %reduce-scatter.29.cloned.1.call-done = bf16[96,6]{1,0:T(8,128)(2,1)} async-done(((bf16[768,6]{1,0:T(8,128)(2,1)}), bf16[96,6]{1,0:T(8,128)(2,1)}) %reduce-scatter.29.cloned.1.call-update) | async-done | bytes 1168
  2332.4 29.8 %reduce-scatter.25.cloned.1.call-done = bf16[96,20]{1,0:T(8,128)(2,1)} async-done(((bf16[768,20]{1,0:T(8,128)(2,1)}), bf16[96,20]{1,0:T(8,128)(2,1)}) %reduce-scatter.25.cloned.1.call-update) | async-done | bytes 3856
  2381.4 99.3 %all-reduce.22.cloned.1.call-done = (bf16[2,768,96]{1,0,2:T(2,128)(2,1)}, bf16[2,768,192]{1,0,2:T(2,128)(2,1)}, bf16[2,768,288]{1,2,0:T(8,128)(2,1)}, bf16[2,96,...) async-done(((bf16[2,768,96]{1,0,2:T(2,128)(2,1)}, bf16[2,768,192]{1,0,2:T(2,128)(2,1)}, ...) | async-done | bytes 4718608 | tf_op jit(solution)/shard_map/psum | solution.py:383
  (911 shorter events, 827.5 us)
Async XLA Ops:
  7.2 436.8 %all-gather.3.cloned.1.call-start = ((), (), s32[]{:S(2)}) async-start(), calls=%async_computation.8 | async-start | bytes 7077888 | tf_op jit(solution)/shard_map/all_gather | solution.py:197
  21.2 11.8 collective-permute-start
  26.3 6.7 collective-permute-start.1
  32.9 438.7 %copy-start.140 = (f32[768]{0:T(1024)}, f32[768]{0:T(1024)S(1)}, u32[]{:S(2)}) copy-start(f32[768]{0:T(1024)S(1)} %get-tuple-element.277) | copy-start | bytes 9220
  32.9 459.3 %copy-start.153 = (f32[768]{0:T(1024)}, f32[768]{0:T(1024)S(1)}, u32[]{:S(2)}) copy-start(f32[768]{0:T(1024)S(1)} %get-tuple-element.278) | copy-start | bytes 9220
  32.9 498.1 %copy-start.142 = (f32[768]{0:T(1024)}, f32[768]{0:T(1024)S(1)}, u32[]{:S(2)}) copy-start(f32[768]{0:T(1024)S(1)} %get-tuple-element.279) | copy-start | bytes 9220
  32.9 499.5 %copy-start.156 = (f32[768]{0:T(1024)}, f32[768]{0:T(1024)S(1)}, u32[]{:S(2)}) copy-start(f32[768]{0:T(1024)S(1)} %get-tuple-element.168) | copy-start | bytes 9220
  32.9 922.8 %copy-start.144 = (f32[768]{0:T(1024)}, f32[768]{0:T(1024)S(1)}, u32[]{:S(2)}) copy-start(f32[768]{0:T(1024)S(1)} %get-tuple-element.280) | copy-start | bytes 9220
  45.8 425.8 %copy-start.4 = (f32[4,128,768]{2,1,0:T(8,128)}, f32[4,128,768]{2,1,0:T(8,128)S(1)}, u32[]{:S(2)}) copy-start(f32[4,128,768]{2,1,0:T(8,128)S(1)} %get-tuple-element.242) | copy-start | bytes 4718596
  66.9 19.6 collective-permute-start.2
  376.8 551.3 %all-gather.5.cloned.1.call-start = ((), (), s32[]{:S(2)}) async-start(), calls=%async_computation.9 | async-start | bytes 7077888 | tf_op jit(solution)/shard_map/all_gather | solution.py:197
  508.7 7.8 collective-permute-start.3
  513.6 5.6 collective-permute-start.4
  552.8 18.4 collective-permute-start.5
  862.2 298.2 %all-reduce.20.cloned.1.call-start = ((), (), s32[]{:S(2)}) async-start(), calls=%async_computation.20 | async-start | bytes 12582912
  1025.2 574.9 %all-reduce.18.cloned.1.call-start = ((), (), s32[]{:S(2)}) async-start(), calls=%async_computation.19 | async-start | bytes 12582912
  1251.8 11.9 collective-permute-start.6
  1303.6 8.5 collective-permute-start.7
  1306.7 5.8 collective-permute-start.8
  1447.1 540.5 %all-reduce.16.cloned.1.call-start = ((), (), s32[]{:S(2)}) async-start(), calls=%async_computation.18 | async-start | bytes 14155776
  1691.6 11.8 collective-permute-start.9
  1743.2 271.5 %reduce-scatter.27.cloned.1.call-start = ((), (), s32[]{:S(2)}) async-start(), calls=%async_computation.15 | async-start | bytes 10616832
  1796.6 254.8 %reduce-scatter.21.cloned.1.call-start = ((), (), s32[]{:S(2)}) async-start(), calls=%async_computation.12 | async-start | bytes 2654208 | tf_op jit(solution)/shard_map/reduce_scatter | solution.py:364
  1802.3 287.7 %reduce-scatter.19.cloned.1.call-start = ((), (), s32[]{:S(2)}) async-start(), calls=%async_computation.11 | async-start | bytes 2654208 | tf_op jit(solution)/shard_map/reduce_scatter | solution.py:352
  1832.8 335.9 %reduce-scatter.17.cloned.1.call-start = ((), (), s32[]{:S(2)}) async-start(), calls=%async_computation.10 | async-start | bytes 7962624 | tf_op jit(solution)/shard_map/reduce_scatter | solution.py:349
  1847.9 12.4 collective-permute-start.10
  1851.3 9.1 collective-permute-start.11
  1952.4 316.4 %reduce-scatter.23.cloned.1.call-start = ((), (), s32[]{:S(2)}) async-start(), calls=%async_computation.13 | async-start | bytes 10616832 | tf_op jit(solution)/shard_map/reduce_scatter | solution.py:370
  1972.4 327.8 %reduce-scatter.31.cloned.1.call-start = ((), (), s32[]{:S(2)}) async-start(), calls=%async_computation.17 | async-start | bytes 221184
  1977.4 354.0 %reduce-scatter.29.cloned.1.call-start = ((), (), s32[]{:S(2)}) async-start(), calls=%async_computation.16 | async-start | bytes 221184
  1978.9 383.3 %reduce-scatter.25.cloned.1.call-start = ((), (), s32[]{:S(2)}) async-start(), calls=%async_computation.14 | async-start | bytes 221184
  1987.6 493.2 %all-reduce.22.cloned.1.call-start = ((), (), s32[]{:S(2)}) async-start(), calls=%async_computation.21 | async-start | bytes 9437184 | tf_op jit(solution)/shard_map/psum | solution.py:383
  (246 other events, 6484.0 us)
Sparse Core Ops, SparseCore 0:
  376.9 66.9 all-gather.2
  862.3 65.7 all-gather.4
  1025.3 135.0 all-reduce.19
  1447.3 152.7 all-reduce.17
  1743.3 169.4 all-reduce.15
  1914.9 99.7 reduce-scatter.26
  2017.0 34.4 reduce-scatter.20
  2054.4 35.5 reduce-scatter.18
  2092.3 76.3 reduce-scatter.16
  2170.8 97.8 reduce-scatter.22
  2271.6 28.6 reduce-scatter.30
  2303.0 28.4 reduce-scatter.28
  2333.7 28.4 reduce-scatter.24
  2367.8 112.9 all-reduce.21
where the time goes:
time: 2540 us; the launch traced here: 2500 us
  local copies, waits for them, and re-layouts  1050 us (41%)
  waiting for transfers between devices  863 us (34%)
  other arithmetic  281 us (11%)
  matrix products  216 us (9%)
  starting transfers between devices  60.3 us (2%)
    slice x8, local copies, waits for them, and re-layouts, apply_taps(): extended[:, tap_at:tap_at + 4 * pool_rows:4] * taps[:, tap_at]  428 us
    unnamed x21, waiting for transfers between devices  385 us
    unnamed x545, local copies, waits for them, and re-layouts  130 us
    all_gather x2, waiting for transfers between devices, per_device(): forward_all_pooled = lax.all_gather(pooled, 'seq', axis=1, tiled=True)  127 us
    slice x2, local copies, waits for them, and re-layouts, apply_taps(): total = extended[:, 0:4 * pool_rows:4] * taps[:, 0]  106 us
    reduce_scatter x1, waiting for transfers between devices, per_device(): lax.psum_scatter(stacked[7].astype(jnp.bfloat16), 'seq', scatter_dimensio...  100 us
    psum x1, waiting for transfers between devices, per_device(): lax.psum(shards_all[2].astype(jnp.bfloat16), 'doc').astype(jnp.float32)  99.3 us
    reduce_scatter x1, waiting for transfers between devices, per_device(): lax.psum_scatter(stacked[0].astype(jnp.bfloat16), 'seq', scatter_dimensio...  78.7 us
  transfers between devices with their start and end apart: 26, of which 17 were waited for; matrix products, arithmetic and copies ran while one was open for 12% of the time, Pallas kernels for 0%

commit v1 on v0

--- a/solution.py
+++ b/solution.py
@@ -1,15 +1,1613 @@
+from types import SimpleNamespace
+
 import jax
 import jax.numpy as jnp
 from jax import lax
+from jax.experimental import pallas as pl
+from jax.experimental.pallas import tpu as pltpu
 from jax.sharding import PartitionSpec as P
 
 HD = 64
 LOCAL_WIN = 128
 POOL_WIN = 512
-
-
 EPSILON = 1e-05
 MASKED = -1e30
+F32 = jnp.float32
+BF16 = jnp.bfloat16
+MESH = pl.DeviceIdType.MESH
+ANY = pl.BlockSpec(memory_space=pl.ANY)
+VMEM = pl.BlockSpec(memory_space=pltpu.VMEM)
+VMEM_LIMIT = 60 * 1024 * 1024
+
+
+def dot_nn(left, right):
+    return jnp.dot(left, right, preferred_element_type=F32)
+
+
+def dot_nt(left, right):
+    return lax.dot_general(left, right, (((1,), (1,)), ((), ())), preferred_element_type=F32)
+
+
+def dot_tn(left, right):
+    return lax.dot_general(left, right, (((0,), (0,)), ((), ())), preferred_element_type=F32)
+
+
+def loop(count, body):
+    def step(i, carry):
+        body(i)
+        return carry
+
+    lax.fori_loop(0, count, step, 0)
+
+
+def aligned(index, size):
+    return pl.ds(pl.multiple_of(index * size, size), size)
+
+
+class Copies:
+    def __init__(self, sems):
+        self.sems = sems
+        self.used = 0
+
+    def start(self, source, target):
+        copy = pltpu.make_async_copy(source, target, self.sems.at[self.used])
+        self.used += 1
+        copy.start()
+        return copy
+
+
+class Links:
+    def __init__(self, send, recv):
+        self.send, self.recv = send, recv
+        self.used = 0
+
+    def take(self):
+        self.used += 1
+        return self.used - 1
+
+    def start(self, source, target, device):
+        at = self.take()
+        copy = pltpu.make_async_remote_copy(
+            src_ref=source,
+            dst_ref=target,
+            send_sem=self.send.at[at],
+            recv_sem=self.recv.at[at],
+            device_id=device,
+            device_id_type=MESH,
+        )
+        copy.start()
+        return copy
+
+
+def greet(devices):
+    barrier = pltpu.get_barrier_semaphore()
+    for device in devices:
+        pl.semaphore_signal(barrier, inc=1, device_id=device, device_id_type=MESH)
+    pl.semaphore_wait(barrier, len(devices))
+
+
+class Regroup:
+    def __init__(self, copies, links, source, target, gather):
+        self.doc, self.me = lax.axis_index("doc"), lax.axis_index("seq")
+        self.source, self.target = source, target
+        self.gather = gather
+        self.copies, self.links = copies, links
+        self.local = copies.used
+        copies.used += 1
+        self.first = links.used
+        links.used += 4
+
+    def _to(self, i):
+        if self.gather:
+            return 2 * i + self.me // 4, self.me % 4
+        return 4 * (self.me % 2) + i, self.me // 2
+
+    def _from(self, i):
+        if self.gather:
+            return 4 * (self.me % 2) + i
+        return 2 * i + self.me // 4
+
+    def _remote(self, i, slot, device):
+        return pltpu.make_async_remote_copy(
+            src_ref=self.source.at[i],
+            dst_ref=self.target.at[slot],
+            send_sem=self.links.send.at[self.first + i],
+            recv_sem=self.links.recv.at[self.first + slot],
+            device_id=(self.doc, device),
+            device_id_type=MESH,
+        )
+
+    def _local(self, i, slot):
+        return pltpu.make_async_copy(
+            self.source.at[i], self.target.at[slot], self.copies.sems.at[self.local]
+        )
+
+    def start(self):
+        for i in range(4):
+            device, slot = self._to(i)
+
+            @pl.when(device == self.me)
+            def _():
+                self._local(i, slot).start()
+
+            @pl.when(device != self.me)
+            def _():
+                self._remote(i, slot, device).start()
+
+    def wait(self):
+        for i in range(4):
+            device, slot = self._to(i)
+
+            @pl.when(device == self.me)
+            def _():
+                self._local(i, slot).wait()
+
+            @pl.when(device != self.me)
+            def _():
+                self._remote(i, slot, device).wait_send()
+
+        for i in range(4):
+
+            @pl.when(self._from(i) != self.me)
+            def _():
+                self._remote(i, i, self._from(i)).wait_recv()
+
+
+def regroup_peers():
+    me = lax.axis_index("seq")
+    return [2 * i + me // 4 for i in range(4)], [4 * (me % 2) + i for i in range(4)]
+
+
+def greet_regroup(others):
+    doc, me = lax.axis_index("doc"), lax.axis_index("seq")
+    barrier = pltpu.get_barrier_semaphore()
+    to, back = regroup_peers()
+    for device in to + back:
+
+        @pl.when(device != me)
+        def _():
+            pl.semaphore_signal(barrier, inc=1, device_id=(doc, device), device_id_type=MESH)
+
+    for device in others:
+        pl.semaphore_signal(barrier, inc=1, device_id=device, device_id_type=MESH)
+    inside = me // 4 == me % 2
+    pl.semaphore_wait(barrier, len(others) + jnp.where(inside, 6, 8))
+
+
+def split_masks(width):
+    lane = lax.broadcasted_iota(jnp.int32, (1, 2 * HD), 1)
+    low = (lane < HD).astype(F32)
+    return low, 1.0 - low
+
+
+def by_head(rows, low, high, factor):
+    wide = rows.astype(F32) * factor
+    return jnp.concatenate([wide * low, wide * high], 0).astype(BF16)
+
+
+def from_heads(stacked, low, high):
+    rows = stacked.shape[0] // 2
+    return stacked[:rows] * low + stacked[rows:] * high
+
+
+def attend_blocks(queries, key_rows, value_rows, bias):
+    low, high = split_masks(2 * HD)
+    wide_bias = jnp.concatenate([bias, bias], 0)
+    scores = [
+        dot_nt(by_head(query, low, high, HD**-0.5), key) + wide_bias
+        for query, key in zip(queries, key_rows)
+    ]
+    soft = []
+    for score in scores:
+        raised = jnp.exp(score - jnp.max(score, -1, keepdims=True))
+        soft.append((raised.astype(BF16), 1.0 / jnp.sum(raised, -1, keepdims=True)))
+    return [
+        from_heads(dot_nn(raised, value) * share, low, high).astype(BF16)
+        for (raised, share), value in zip(soft, value_rows)
+    ]
+
+
+def local_bias(at, blocks, length_first, length_last, rows, half):
+    shape = (rows, rows + 2 * half)
+    query = lax.broadcasted_iota(jnp.int32, shape, 0)
+    key = lax.broadcasted_iota(jnp.int32, shape, 1)
+    first = jnp.where(length_first & (at == 0), half, 0)
+    last = jnp.where(length_last & (at == blocks - 1), rows + half, rows + 2 * half)
+    seen = (key >= query) & (key <= query + 2 * half) & (key >= first) & (key < last)
+    return jnp.where(seen, 0.0, MASKED).astype(F32)
+
+
+def norm_rows(summed, gain, shift):
+    centre = summed - jnp.mean(summed, -1, keepdims=True)
+    spread = jnp.mean(centre * centre, -1, keepdims=True)
+    rate = lax.rsqrt(spread + EPSILON)
+    plain = centre * rate
+    return plain, rate, plain * gain + shift
+
+
+def gelu_rows(u):
+    z = jnp.abs(u) * (0.5**0.5)
+    t = 1.0 / (1.0 + 0.3275911 * z)
+    series = 1.061405429 * t - 1.453152027
+    series = series * t + 1.421413741
+    series = series * t - 0.284496736
+    series = series * t + 0.254829592
+    bell = jnp.exp(-(z * z))
+    tail = 0.5 * series * t * bell
+    share = jnp.where(u < 0, tail, 1.0 - tail)
+    return u * share, share + u * bell * 0.3989422804014327
+
+
+def vmem(shape, kind=BF16):
+    return pltpu.VMEM(shape, kind)
+
+
+class Scratch:
+    def __init__(self):
+        self.names, self.shapes = [], []
+
+    def add(self, tag="", **shapes):
+        for name, shape in shapes.items():
+            self.names.append(tag + name)
+            self.shapes.append(shape)
+
+    def plane(self, tag, block):
+        first = vmem((2, 2, 4, 2) + block)
+        second, total = vmem((2, 2, 4) + block), vmem((2, 4, 2) + block)
+        self.add(tag, kept=first, got1=first, got2=second, total=total)
+
+    def line(self, tag, block):
+        whole = vmem((2, 2, 2, 2) + block)
+        self.add(tag, own=vmem((2, 2) + block), got=vmem((2, 3, 2) + block), whole=whole)
+
+    def core(self, tag, block):
+        group = vmem((2, 4, 2, 2, 2) + block)
+        self.add(tag, send=group, mine=group, got=group)
+
+    def sems(self, loads, saves, links):
+        dma = pltpu.SemaphoreType.DMA
+        self.add(load_sems=dma((loads,)), save_sems=dma((saves,)))
+        self.add(send_sems=dma((links,)), recv_sems=dma((links,)))
+
+    def bring(self, args, **arrays):
+        for name, array in arrays.items():
+            args[name] = (array, ANY)
+            self.names.append("v_" + name)
+            self.shapes.append(pltpu.VMEM(array.shape, array.dtype))
+
+
+class Kernel:
+    def __init__(self, names, refs):
+        self.__dict__.update(zip(names, refs))
+        assert len(names) == len(refs)
+        self.loads = Copies(self.load_sems)
+        self.saves = Copies(self.save_sems)
+        self.links = Links(self.send_sems, self.recv_sems)
+        self.waits = []
+
+    def load(self, source, target):
+        return self.loads.start(source, target)
+
+    def load_all(self, names):
+        return {name: self.load(getattr(self, name), getattr(self, "v_" + name)) for name in names}
+
+    def save(self, source, target):
+        self.waits.append(self.saves.start(source, target))
+
+    def done(self):
+        for wait in self.waits:
+            wait.wait()
+
+
+def run_kernel(body, name, collective, args, outs, scratch):
+    names = list(args) + list(outs) + scratch.names
+
+    def kernel(*refs):
+        body(Kernel(names, refs))
+
+    made = pl.pallas_call(
+        kernel,
+        out_shape=[jax.ShapeDtypeStruct(shape, kind) for shape, kind in outs.values()],
+        in_specs=[spec for _, spec in args.values()],
+        out_specs=[ANY] * len(outs),
+        scratch_shapes=scratch.shapes,
+        compiler_params=pltpu.CompilerParams(
+            collective_id=collective,
+            has_side_effects=collective is not None,
+            vmem_limit_bytes=VMEM_LIMIT,
+        ),
+        name=name,
+    )(*(array for array, _ in args.values()))
+    return SimpleNamespace(**dict(zip(outs, made)))
+
+
+def turn(source, target):
+    for i in range(0, source.shape[1], 128):
+        target[i : i + 128] = source[:, i : i + 128].T
+
+
+GAIN, SHIFT, TAPS = 0, 3, 6
+
+
+def small_row(k, layer, row, lane=None, count=None):
+    lanes = slice(None) if lane is None else slice(lane, lane + count)
+    return k.small[layer, row : row + 1, lanes]
+
+
+def fill_pooled_bias(k, rows, core):
+    doc = lax.axis_index("seq") // 2
+    places = k.places[pl.ds(doc, 1)]
+    slot = lax.broadcasted_iota(jnp.int32, (128, places.shape[1]), 1)
+    column = lax.broadcasted_iota(jnp.int32, (128, rows // 2), 1)
+    for i in range(0, rows, 128):
+        here = core * rows + i
+        position = lax.broadcasted_iota(jnp.int32, (128, places.shape[1]), 0) + here
+        hit = (position == places) & (slot < k.counts[doc])
+        question = jnp.max(hit.astype(F32), -1, keepdims=True)
+        own = (lax.broadcasted_iota(jnp.int32, (128, rows // 2), 0) + here) // 4
+        near = jnp.where(jnp.abs(column - own) <= POOL_WIN // 2, 1.0, 0.0)
+        bias = jnp.where(near + question > 0.5, 0.0, MASKED).astype(F32)
+        k.pbias[i : i + 128] = bias
+        k.pbias_t[:, i : i + 128] = bias.T
+
+
+def forward(k, layer, first, last, rows, width, ff):
+    half = LOCAL_WIN // 2
+    pool = rows // 4
+    blocks = rows // 128
+    pairs = width // (2 * HD)
+    lanes_of = [slice(2 * HD * pair, 2 * HD * (pair + 1)) for pair in range(pairs)]
+    values_of = [slice(width + s.start, width + s.stop) for s in lanes_of]
+    core = lax.axis_index("seq") % 2
+    sibling = axis_peers()[0]
+    links = k.links
+
+    def weight(source, target):
+        return k.load(source.at[layer], target)
+
+    got_small = k.load(k.small_in, k.small)
+    if not first:
+        got_x = k.load(k.x_in, k.xf)
+    got = [weight(k.w_local, k.wl)]
+    if first:
+        greet_regroup([sibling])
+        incoming = Regroup(k.loads, links, k.x_in, k.x, True)
+        incoming.start()
+        background = Regroup(k.loads, links, k.grad_in, k.grad_got, True)
+        fill_pooled_bias(k, rows, core)
+        k.save(k.pbias, k.o_pbias)
+        k.save(k.pbias_t, k.o_pbias_t)
+    else:
+        greet([sibling])
+    for i in range(blocks):
+        k.lbias[i] = local_bias(i, blocks, core == 0, core == 1, 128, half)
+    k.kvf[:, pl.ds(0, 8)] = jnp.zeros((2 * width // 128, 8, 128), F32)
+
+    if first:
+        incoming.wait()
+        xrows = k.x.reshape(rows, width)
+    else:
+        got_x.wait()
+        xrows = k.x
+        for i in range(0, rows, 128):
+            k.x[i : i + 128] = k.xf[i : i + 128].astype(BF16)
+    k.save(k.x, k.o_x)
+    got += [weight(k.w_mix, k.wm), weight(k.w_pooled, k.wp)]
+    if not first:
+        got_bias = k.load(k.pbias_in, k.pbias)
+
+    got[0].wait()
+    for i in range(0, 2 * width, 256):
+        k.kv[half : half + rows, i : i + 256] = dot_nn(
+            xrows[...], k.wl[:, width + i : width + i + 256]
+        ).astype(BF16)
+    rim = links.start(
+        k.kv.at[pl.ds(pl.multiple_of(half + (rows - half) * (1 - core), half), half)],
+        k.halo,
+        sibling,
+    )
+    for i in range(0, width, 256):
+        k.q[:, i : i + 256] = dot_nn(xrows[...], k.wl[:, i : i + 256]).astype(BF16)
+    k.save(k.q, k.o_q)
+    rim.wait()
+    k.kv[pl.ds(pl.multiple_of((rows + half) * (1 - core), half), half)] = k.halo[...]
+    k.kv[pl.ds(pl.multiple_of((rows + half) * core, half), half)] = jnp.zeros_like(k.halo)
+    k.save(k.kv, k.o_kv)
+
+    def attend_local(i):
+        here, seen = aligned(i, 128), pl.ds(pl.multiple_of(i * 128, 128), 128 + 2 * half)
+        mixed = attend_blocks(
+            [k.q[here, lanes] for lanes in lanes_of],
+            [k.kv[seen, lanes] for lanes in lanes_of],
+            [k.kv[seen, lanes] for lanes in values_of],
+            k.lbias[i],
+        )
+        for lanes, part in zip(lanes_of, mixed):
+            k.a[here, lanes] = part
+
+    loop(blocks, attend_local)
+    k.save(k.a, k.o_a)
+    got += [weight(k.w_mix2, k.wm2), weight(k.w_up, k.wu), weight(k.w_down, k.wd)]
+    if first:
+        background.start()
+    got_small.wait()
+
+    def mix_norm(at_norm, mixed, weight, residual, plain_ref, rate_ref, full_ref, narrow_ref):
+        gain, shift = small_row(k, layer, GAIN + at_norm), small_row(k, layer, SHIFT + at_norm)
+        for i in range(0, rows, 128):
+            at = slice(i, i + 128)
+            update = k.acc[at] if weight is None else dot_nn(mixed[at], weight[...])
+            plain, rate, full = norm_rows(residual[at].astype(F32) + update, gain, shift)
+            plain_ref[at] = plain.astype(BF16)
+            rate_ref[at] = jnp.broadcast_to(rate, (128, 128))
+            if full_ref is not None:
+                full_ref[at] = full
+            if narrow_ref is not None:
+                narrow_ref[at] = full.astype(BF16)
+
+    got[1].wait()
+    mix_norm(0, k.a, k.wm, xrows if first else k.xf, k.xh, k.rt, k.x1f, k.x1)
+    k.save(k.xh, k.o_xh1)
+    k.save(k.rt, k.o_r1)
+    k.save(k.x1, k.o_x1)
+
+    got[2].wait()
+    for i in range(0, 2 * width, 256):
+        part = dot_nn(k.x1[...], k.wp[:, width + i : width + i + 256]).astype(BF16)
+        k.kv2[:, i : i + 256] = part
+        k.kvf[i // 128, 8 : 8 + rows] = part[:, :128].astype(F32)
+        k.kvf[i // 128 + 1, 8 : 8 + rows] = part[:, 128:].astype(F32)
+    k.save(k.kv2, k.o_kv2)
+    for chunk in range(2 * width // 128):
+        side, lane = chunk * 128 // width, chunk * 128 % width
+        lanes = slice(chunk * 128, chunk * 128 + 128)
+        total = jnp.zeros((pool, 128), F32)
+        tail = jnp.zeros((1, 128), F32)
+        for t in range(5):
+            tap = small_row(k, layer, TAPS + 5 * side + t, lane, 128)
+            total = total + k.kvf[chunk, pl.ds(6 + t, pool, stride=4)] * tap
+            if t < 2:
+                tail = tail + k.kvf[chunk, pl.ds(6 + rows + t, 1)] * tap
+        k.kp_own[:, lanes] = total.astype(BF16)
+        k.aux_own[0:8, lanes] = jnp.broadcast_to(tail, (8, 128))
+        k.aux_own[8:16, lanes] = total[:8]
+    pooled_out = links.start(k.kp_own, k.kp_got, sibling)
+    aux_out = links.start(k.aux_own, k.aux_got, sibling)
+    for i in range(0, width, 256):
+        k.q2[:, i : i + 256] = dot_nn(k.x1[...], k.wp[:, i : i + 256]).astype(BF16)
+    k.save(k.q2, k.o_q2)
+    if not first:
+        got_bias.wait()
+    pooled_out.wait()
+    aux_out.wait()
+    k.pk[pl.ds(pl.multiple_of(core * pool, pool), pool)] = k.kp_own[...]
+    k.pk[pl.ds(pl.multiple_of((1 - core) * pool, pool), pool)] = k.kp_got[...]
+    tail = jnp.where(core == 0, k.aux_own[0:1], k.aux_got[0:1])
+    head = jnp.where(core == 0, k.aux_got[8:9], k.aux_own[8:9])
+    edge = lax.broadcasted_iota(jnp.int32, (16, 1), 0) == 0
+    k.pk[pool : pool + 16] = jnp.where(
+        edge, jnp.broadcast_to(head + tail, (16, 2 * width)), k.pk[pool : pool + 16].astype(F32)
+    ).astype(BF16)
+    k.save(k.pk, k.o_pk)
+
+    def attend_pooled(i):
+        here = aligned(i, 128)
+        mixed = attend_blocks(
+            [k.q2[here, lanes] for lanes in lanes_of],
+            [k.pk[:, lanes] for lanes in lanes_of],
+            [k.pk[:, lanes] for lanes in values_of],
+            k.pbias[here],
+        )
+        for lanes, part in zip(lanes_of, mixed):
+            k.b[here, lanes] = part
+
+    loop(blocks, attend_pooled)
+    k.save(k.b, k.o_b)
+    got[3].wait()
+    mix_norm(1, k.b, k.wm2, k.x1f, k.xh2, k.rt2, k.x1f, k.x2)
+    k.save(k.xh2, k.o_xh2)
+    k.save(k.rt2, k.o_r2)
+    k.save(k.x2, k.o_x2)
+
+    got[4].wait()
+    got[5].wait()
+    part, up = 512, (k.up_a, k.up_b)
+    count = ff // part
+
+    def expand(i):
+        up[i % 2][...] = dot_nn(k.x2[...], k.wu[:, i * part : (i + 1) * part])
+
+    expand(0)
+    for i in range(count):
+        if i + 1 < count:
+            expand(i + 1)
+        lanes = slice(i * part, (i + 1) * part)
+        full, slope = gelu_rows(up[i % 2][...])
+        k.g[:, lanes] = full.astype(BF16)
+        k.gp[:, lanes] = slope.astype(BF16)
+        k.save(k.g.at[:, lanes], k.o_g.at[:, lanes])
+        k.save(k.gp.at[:, lanes], k.o_gp.at[:, lanes])
+        product = dot_nn(full.astype(BF16), k.wd[lanes])
+        if i == 0:
+            k.acc[...] = product
+        else:
+            k.acc[...] += product
+    result = k.out16 if last else k.xf
+    mix_norm(
+        2, None, None, k.x1f, k.xh3, k.rt3, None if last else result, result if last else None
+    )
+    k.save(k.xh3, k.o_xh3)
+    k.save(k.rt3, k.o_r3)
+    k.save(result, k.o_out)
+    if first:
+        background.wait()
+        k.save(k.grad_got, k.o_grad)
+    k.done()
+
+
+def forward_call(layer, first, last, x_in, small, weights, extra):
+    width, ff = weights[0].shape[1], weights[4].shape[2]
+    rows = x_in.shape[0] * x_in.shape[1] if first else x_in.shape[0]
+    half, pool = LOCAL_WIN // 2, rows // 4
+    x_shape = (4, rows // 4, width) if first else (rows, width)
+    local, mixer, pooled, mixer2, up, down = ((weight, ANY) for weight in weights)
+    args = dict(x_in=(x_in, ANY), small_in=(small, ANY), w_local=local, w_mix=mixer)
+    args.update(w_pooled=pooled, w_mix2=mixer2, w_up=up, w_down=down)
+    wide, kv = ((rows, width), BF16), ((rows + 2 * half, 2 * width), BF16)
+    rate, feed, full = ((rows, 128), F32), ((rows, ff), BF16), ((rows, width), F32)
+    outs = dict(o_x=(x_shape, BF16), o_q=wide, o_kv=kv, o_a=wide, o_xh1=wide, o_r1=rate)
+    outs.update(o_x1=wide, o_q2=wide, o_kv2=((rows, 2 * width), BF16))
+    outs.update(o_pk=((2 * pool, 2 * width), BF16), o_b=wide, o_xh2=wide, o_r2=rate)
+    outs.update(o_x2=wide, o_g=feed, o_gp=feed, o_xh3=wide, o_r3=rate)
+    outs.update(o_out=wide if last else full)
+    s = Scratch()
+    wl, wm, wp, wm2, wu, wd = (vmem(weight.shape[1:]) for weight in weights)
+    s.add(wl=wl, wm=wm, wp=wp, wm2=wm2, wu=wu, wd=wd)
+    wide, full, rate, feed = (vmem(*shape) for shape in (wide, full, rate, feed))
+    s.add(small=vmem(small.shape, F32), x=vmem(x_shape))
+    s.add(q=wide, a=wide, xh=wide, x1=wide, q2=wide, b=wide, xh2=wide, x2=wide, xh3=wide)
+    s.add(xf=full, x1f=full, acc=full, rt=rate, rt2=rate, rt3=rate, g=feed, gp=feed)
+    part, pooled = vmem((rows, 512), F32), vmem((pool, 2 * width))
+    s.add(up_a=part, up_b=part, kv=vmem(*kv), kv2=vmem((rows, 2 * width)))
+    s.add(kvf=vmem((2 * width // 128, rows + 8, 128), F32), pk=vmem((2 * pool, 2 * width)))
+    aux = vmem((16, 2 * width), F32)
+    s.add(halo=vmem((half, 2 * width)), kp_own=pooled, kp_got=pooled, aux_own=aux, aux_got=aux)
+    s.add(lbias=vmem((rows // 128, 128, 128 + 2 * half), F32))
+    s.add(pbias=vmem((rows, 2 * pool), F32))
+    if last:
+        s.add(out16=wide)
+    if first:
+        counts, places, grad_in = extra
+        args.update(counts=(counts, pl.BlockSpec(memory_space=pltpu.SMEM)))
+        args.update(places=(places, VMEM), grad_in=(grad_in, ANY))
+        outs.update(o_grad=(grad_in.shape, BF16))
+        outs.update(o_pbias=((rows, 2 * pool), F32), o_pbias_t=((2 * pool, rows), F32))
+        s.add(grad_got=vmem(grad_in.shape), pbias_t=vmem((2 * pool, rows), F32))
+    else:
+        args.update(pbias_in=(extra, ANY))
+    s.sems(16, 40, 12)
+    return run_kernel(
+        lambda k: forward(k, layer, first, last, rows, width, ff),
+        "forward_%d" % layer,
+        layer,
+        args,
+        outs,
+        s,
+    )
+
+
+def axis_peers():
+    doc, me = lax.axis_index("doc"), lax.axis_index("seq")
+    core, z = me % 2, me // 2
+    along = (z + 1 - 2 * (z % 2), z + 2 - 4 * (z // 2), 3 - z)
+    return (
+        (doc, me + 1 - 2 * core),
+        (doc + 1 - 2 * (doc % 2), me),
+        (doc + 2 - 4 * (doc // 2), me),
+        [(doc, 2 * other + core) for other in along],
+        along,
+    )
+
+
+BOTH = (0, 1)
+
+
+class CoreSum:
+    def __init__(self, k, tag):
+        self.links = k.links
+        self.send, self.own, self.got = (getattr(k, tag + part) for part in ("send", "mine", "got"))
+        self.copy = {}
+
+    def start(self, part):
+        self.copy[part] = self.links.start(
+            self.send.at[part], self.got.at[part], axis_peers()[0]
+        )
+
+    def finish(self, *parts):
+        for part in parts or BOTH:
+            self.copy[part].wait()
+
+            def add(z):
+                self.own[part, z] += self.got[part, z]
+
+            loop(4, add)
+
+
+class PlaneSum:
+    def __init__(self, k, tag, source):
+        self.links, self.copies, self.source = k.links, k.loads, source
+        self.kept, self.got1, self.got2, self.total = (
+            getattr(k, tag + part) for part in ("kept", "got1", "got2", "total")
+        )
+        doc = lax.axis_index("doc")
+        self.x, self.y = doc % 2, doc // 2
+        self.copy = {}
+
+    def start(self, *parts):
+        _, across, up, _, _ = axis_peers()
+        x, y = self.x, self.y
+        for part in parts or BOTH:
+            source, got = self.source.at[part], self.got1.at[part]
+            self.copy[part] = [
+                self.links.start(source.at[:, 0, :, 1 - x], got.at[0], across),
+                self.links.start(source.at[:, 1, 1 - y], got.at[1], up),
+                self.copies.start(source.at[:, 0, :, x], self.kept.at[part, 0]),
+                self.copies.start(source.at[:, 1, y], self.kept.at[part, 1]),
+            ]
+
+    def middle(self, *parts):
+        _, across, up, _, _ = axis_peers()
+        for part in parts or BOTH:
+            for copy in self.copy[part]:
+                copy.wait()
+
+            def add(half):
+                self.kept[part, half] += self.got1[part, half]
+
+            loop(2, add)
+            kept, got = self.kept.at[part], self.got2.at[part]
+            self.copy[part] = [
+                self.links.start(kept.at[0, :, 1 - self.y], got.at[0], up),
+                self.links.start(kept.at[1, :, 1 - self.x], got.at[1], across),
+            ]
+
+    def finish(self, *parts):
+        for part in parts or BOTH:
+            for copy in self.copy[part]:
+                copy.wait()
+            for z in range(4):
+                self.total[part, z, 0] = self.kept[part, 0, z, self.y] + self.got2[part, 0, z]
+                self.total[part, z, 1] = self.kept[part, 1, z, self.x] + self.got2[part, 1, z]
+
+
+class LineSum:
+    def __init__(self, k, tag, source):
+        self.links, self.copies, self.source = k.links, k.loads, source
+        self.whole = getattr(k, tag + "whole")
+        if hasattr(k, tag + "own"):
+            self.own, self.got = getattr(k, tag + "own"), getattr(k, tag + "got")
+        doc = lax.axis_index("doc")
+        self.x, self.y = doc % 2, doc // 2
+        self.copy = {}
+
+    def start(self, *parts):
+        _, _, _, line, along = axis_peers()
+        for part in parts or BOTH:
+            source = self.source.at[part]
+            self.copy[part] = [
+                self.links.start(source.at[other], self.got.at[part, i], device)
+                for i, (other, device) in enumerate(zip(along, line))
+            ]
+            self.copy[part].append(
+                self.copies.start(source.at[lax.axis_index("seq") // 2], self.own.at[part])
+            )
+
+    def settle(self, *parts):
+        for part in parts or BOTH:
+            for copy in self.copy[part]:
+                copy.wait()
+            for half in range(2):
+                total = self.own[part, half].astype(F32)
+                for i in range(3):
+                    total = total + self.got[part, i, half].astype(F32)
+                self.whole[part, half, self.y, self.x] = total.astype(BF16)
+
+    def take(self):
+        return [
+            self.copies.start(self.source.at[part, half], self.whole.at[part, half, self.y, self.x])
+            for part in range(2)
+            for half in range(2)
+        ]
+
+    def give(self, k, target):
+        for part in range(2):
+            for half in range(2):
+                k.save(self.whole.at[part, half, self.y, self.x], target.at[part, half])
+
+    def gather(self, *parts):
+        _, across, up, _, _ = axis_peers()
+        for part in parts or BOTH:
+            first = self.whole.at[part, 0, self.y, self.x]
+            second = self.whole.at[part, 1, self.y, self.x]
+            self.copy[part] = [
+                self.links.start(first, first, across),
+                self.links.start(second, second, up),
+            ]
+
+    def middle(self, *parts):
+        for part in parts or BOTH:
+            self.settle(part)
+            self.gather(part)
+
+    def spread(self, *parts):
+        _, across, up, _, _ = axis_peers()
+        for part in parts or BOTH:
+            for copy in self.copy[part]:
+                copy.wait()
+            first = self.whole.at[part, 0, self.y]
+            second = self.whole.at[part, 1, :, self.x]
+            self.copy[part] = [
+                self.links.start(first, first, up),
+                self.links.start(second, second, across),
+            ]
+
+    def finish(self, *parts):
+        for part in parts or BOTH:
+            for copy in self.copy[part]:
+                copy.wait()
+
+
+def norm_back(k, rows, incoming, plain_ref, rate_ref, gain, full, narrow, sums, at_sum):
+    for i in range(0, rows, 128):
+        at = slice(i, i + 128)
+        grad = incoming(at)
+        plain = plain_ref[at].astype(F32)
+        rate = rate_ref[at][:, :1]
+        scaled = grad * gain
+        even = jnp.mean(scaled, -1, keepdims=True)
+        tilt = jnp.mean(scaled * plain, -1, keepdims=True)
+        result = rate * (scaled - even - plain * tilt)
+        full[at] = result
+        narrow[at] = result.astype(BF16)
+        for j, part in enumerate((grad * plain, grad)):
+            part = jnp.sum(part.reshape(16, 8, -1), 0)
+            if i == 0:
+                sums[at_sum + j] = part
+            else:
+                sums[at_sum + j] += part
+
+
+def attend_back_blocks(queries, key_rows, value_rows, grads_mixed, bias):
+    low, high = split_masks(2 * HD)
+    wide_bias = jnp.concatenate([bias, bias], 1)
+    first = []
+    for query, key, value, grad in zip(queries, key_rows, value_rows, grads_mixed):
+        stacked, grads = by_head(query, low, high, HD**-0.5), by_head(grad, low, high, 1.0)
+        first.append((stacked, grads, dot_nt(key, stacked) + wide_bias, dot_nt(value, grads)))
+    second = []
+    for _, _, scores, grad_soft in first:
+        raised = jnp.exp(scores - jnp.max(scores, 0, keepdims=True))
+        soft = raised * (1.0 / jnp.sum(raised, 0, keepdims=True))
+        inner = jnp.sum(soft * grad_soft, 0, keepdims=True)
+        second.append((soft.astype(BF16), (soft * (grad_soft - inner)).astype(BF16)))
+    result = []
+    for (stacked, grads, _, _), (soft, grad_scores), key in zip(first, second, key_rows):
+        grad_queries = from_heads(dot_tn(grad_scores, key), low, high) * HD**-0.5
+        result.append(
+            (grad_queries.astype(BF16), dot_nn(grad_scores, stacked), dot_nn(soft, grads))
+        )
+    return result
+
+
+def local_bias_turned(at, blocks, length_first, length_last, rows, half):
+    shape = (rows + 2 * half, rows)
+    key = lax.broadcasted_iota(jnp.int32, shape, 0)
+    query = lax.broadcasted_iota(jnp.int32, shape, 1)
+    first = jnp.where(length_first & (at == 0), half, 0)
+    last = jnp.where(length_last & (at == blocks - 1), rows + half, rows + 2 * half)
+    seen = (key >= query) & (key <= query + 2 * half) & (key >= first) & (key < last)
+    return jnp.where(seen, 0.0, MASKED).astype(F32)
+
+
+def place_piece(target, part, z, top, bottom):
+    block = target.shape[5:]
+    target[part, z, 0] = top[: 4 * block[0]].reshape((2, 2) + block).astype(BF16)
+    target[part, z, 1, 0] = top[4 * block[0] :].reshape((2,) + block).astype(BF16)
+    target[part, z, 1, 1] = bottom.reshape((2,) + block).astype(BF16)
+
+
+def whole_piece(target, part, z, value):
+    target[part, z] = value.reshape(target.shape[2:]).astype(BF16)
+
+
+def feed_back(k, layer, rows, width, ff, last):
+    core = lax.axis_index("seq") % 2
+    sibling, across, up, line_peers, _ = axis_peers()
+    shard = ff // 8
+    got = k.load_all("dy xh3 r3".split())
+    got_small = k.load(k.small_in, k.small)
+    if not last:
+        greet([sibling, across, up] + line_peers)
+        before, line = PlaneSum(k, "x_", k.x_in), LineSum(k, "z_", k.z_in)
+        before.start()
+        line.start()
+    got.update(k.load_all(["g"]))
+    for name in ("dy", "xh3", "r3"):
+        got[name].wait()
+    got_small.wait()
+    incoming = k.v_dy.reshape(rows, width) if last else k.v_dy
+    norm_back(
+        k,
+        rows,
+        lambda at: incoming[at].astype(F32),
+        k.v_xh3,
+        k.v_r3,
+        small_row(k, layer, GAIN + 2),
+        k.res,
+        k.dn,
+        k.sums,
+        0,
+    )
+    got.update(k.load_all(["gp"]))
+    got_down = k.load(k.w_down.at[layer], k.v_down)
+    turn(k.dn, k.dn_t)
+    got["g"].wait()
+    reduced, expanded = CoreSum(k, "r_"), CoreSum(k, "e_")
+    middle = width // 2
+
+    def reduce_part(part, which, target):
+        rows_of = slice(part * middle, (part + 1) * middle)
+        for z in range(4):
+            lanes = aligned(2 * z + which, shard)
+            whole_piece(target, part, z, dot_nn(k.dn_t[rows_of], k.v_g[:, lanes]))
+
+    def slope_part(first):
+        for i in range(first, first + ff // 2, 512):
+            k.du[:, i : i + 512] = (
+                dot_nt(k.dn[...], k.v_down[i : i + 512]) * k.v_gp[:, i : i + 512].astype(F32)
+            ).astype(BF16)
+
+    reduce_part(0, 1 - core, k.r_send)
+    if last:
+        greet_regroup([sibling, across, up] + line_peers)
+    reduced.start(0)
+    reduce_part(1, 1 - core, k.r_send)
+    reduced.start(1)
+    got.update(k.load_all("x2 xh2 r2".split()))
+    got_up = k.load(k.w_up.at[layer], k.v_up)
+    reduce_part(0, core, k.r_mine)
+    reduce_part(1, core, k.r_mine)
+    if last:
+        outward = Regroup(k.loads, k.links, k.x3, k.regrouped, False)
+        outward.start()
+    got["gp"].wait()
+    got_down.wait()
+    plane = PlaneSum(k, "r_", k.r_mine)
+    if last:
+        reduced.finish(0)
+        plane.start(0)
+    else:
+        before.middle(0)
+    slope_part(0)
+    reduced.finish(*((1,) if last else BOTH))
+    if not last:
+        line.middle()
+        before.middle(1)
+    plane.start(*((1,) if last else BOTH))
+    slope_part(ff // 2)
+    got["x2"].wait()
+    turn(k.v_x2, k.x2_t)
+
+    def expand_part(part, which, target):
+        rows_of = slice(part * middle, (part + 1) * middle)
+        for z in range(4):
+            lanes = aligned(2 * z + which, shard)
+            whole_piece(target, part, z, dot_nn(k.x2_t[rows_of], k.du[:, lanes]))
+
+    for part in BOTH:
+        expand_part(part, 1 - core, k.e_send)
+        expanded.start(part)
+    for part in BOTH:
+        expand_part(part, core, k.e_mine)
+    if not last:
+        line.spread()
+        before.finish()
+        late = LineSum(k, "y_", k.x_total)
+        late.start()
+    else:
+        plane.middle(0)
+    got_up.wait()
+    for i in range(0, width, 256):
+        k.res[:, i : i + 256] += dot_nt(k.du[...], k.v_up[i : i + 256])
+    got["xh2"].wait()
+    got["r2"].wait()
+    norm_back(
+        k,
+        rows,
+        lambda at: k.res[at],
+        k.v_xh2,
+        k.v_r2,
+        small_row(k, layer, GAIN + 1),
+        k.res,
+        k.dn2,
+        k.sums,
+        2,
+    )
+    k.save(k.res, k.o_mid)
+    k.save(k.dn2, k.o_dy2)
+    save_sums(k, 4)
+    expanded.finish()
+    k.save(k.e_mine, k.o_e)
+    plane.middle(*((1,) if last else BOTH))
+    if last:
+        outward.wait()
+        k.save(k.regrouped, k.o_out)
+    else:
+        line.finish()
+        k.save(k.z_whole, k.o_z)
+        late.settle()
+        late.give(k, k.o_y)
+    plane.finish()
+    k.save(k.r_total, k.o_r)
+    k.done()
+
+
+def pooled_back(k, layer, rows, width):
+    core = lax.axis_index("seq") % 2
+    sibling, across, up, line_peers, _ = axis_peers()
+    pool = rows // 4
+    pairs, blocks = width // (2 * HD), rows // 128
+    shard = width // 8
+    got = k.load_all(["dy2"])
+    got_mix = k.load(k.w_mix2.at[layer], k.v_mix2)
+    got_small = k.load(k.small_in, k.small)
+    late = LineSum(k, "y_", k.y_in) if hasattr(k, "y_in") else None
+    if late:
+        got_late = late.take()
+    greet([sibling, across, up] + line_peers)
+    plane, line = PlaneSum(k, "x_", k.x_in), LineSum(k, "z_", k.z_in)
+    if late:
+        for copy in got_late:
+            copy.wait()
+        late.gather()
+    plane.start()
+    line.start()
+    got.update(k.load_all("q2 pk".split()))
+    got_bias = k.load(k.pbias, k.v_pbias)
+    got["dy2"].wait()
+    got_mix.wait()
+    got.update(k.load_all("kv2 b".split()))
+    for i in range(0, width, 256):
+        k.do[:, i : i + 256] = dot_nt(k.v_dy2[...], k.v_mix2[i : i + 256]).astype(BF16)
+    for name in ("q2", "pk"):
+        got[name].wait()
+    k.dkv[...] = jnp.zeros_like(k.dkv)
+    got_bias.wait()
+    got.update(k.load_all("x1 mid xh1 r1".split()))
+    got_proj = k.load(k.w_pooled.at[layer], k.v_pooled)
+    lanes_of = [slice(2 * HD * pair, 2 * HD * (pair + 1)) for pair in range(pairs)]
+    values_of = [slice(width + part.start, width + part.stop) for part in lanes_of]
+
+    def attend_part(i):
+        here = aligned(i, 128)
+        parts = attend_back_blocks(
+            [k.v_q2[here, lanes] for lanes in lanes_of],
+            [k.v_pk[:, lanes] for lanes in lanes_of],
+            [k.v_pk[:, lanes] for lanes in values_of],
+            [k.do[here, lanes] for lanes in lanes_of],
+            k.v_pbias[:, here],
+        )
+        for lanes, values, (grad_q, grad_k, grad_v) in zip(lanes_of, values_of, parts):
+            k.dqkv[here, lanes] = grad_q
+            k.dkv[:, lanes] += grad_k
+            k.dkv[:, values] += grad_v
+
+    loop(blocks, attend_part)
+    k.rim_out[...] = k.dkv[pl.ds(pl.multiple_of((pool - 16) * (1 - core), 16), pool + 16)].astype(
+        BF16
+    )
+    rim = k.links.start(k.rim_out, k.rim_got, sibling)
+    got["b"].wait()
+    turn(k.v_b, k.b_t)
+    got["kv2"].wait()
+    for c in range(2 * width // 128):
+        k.kvf[c] = k.v_kv2[:, pl.ds(c * 128, 128)].astype(F32)
+    got_small.wait()
+    rim.wait()
+    k.total[pl.ds(0, pool)] = (
+        k.dkv[pl.ds(pl.multiple_of(core * pool, pool), pool)]
+        + k.rim_got[pl.ds(pl.multiple_of(core * 16, 16), pool)].astype(F32)
+    )
+    k.total[pl.ds(pool, 8)] = jnp.where(
+        core == 0, k.dkv[pl.ds(pool, 8)] + k.rim_got[pl.ds(pool, 16)].astype(F32)[:8], 0.0
+    )
+
+    for c in range(2 * width // 128):
+        side, lane = c * 128 // width, c * 128 % width
+        lanes = pl.ds(c * 128, 128)
+        own, after = k.total[pl.ds(0, pool), lanes], k.total[pl.ds(1, pool), lanes]
+        rows_at = [pl.ds(j, pool, stride=4) for j in range(4)]
+        kept = [k.kvf[c, at] for at in rows_at]
+        taps = [small_row(k, layer, TAPS + 5 * side + t, lane, 128) for t in range(5)]
+        pairs_of = ((kept[2], after), (kept[3], after), (kept[0], own), (kept[1], own), (kept[2], own))
+        for t, (token, grad) in enumerate(pairs_of):
+            k.tap_sums[side, 8 * t : 8 * t + 8, lane : lane + 128] = jnp.sum(
+                (token * grad).reshape(pool // 8, 8, 128), 0
+            )
+        k.kvf[c, rows_at[0]] = own * taps[2]
+        k.kvf[c, rows_at[1]] = own * taps[3]
+        k.kvf[c, rows_at[2]] = own * taps[4] + after * taps[0]
+        k.kvf[c, rows_at[3]] = after * taps[1]
+        k.dqkv[:, pl.ds(width + c * 128, 128)] = k.kvf[c].astype(BF16)
+    turn(k.dqkv, k.dqkv_t)
+    got["x1"].wait()
+    if late:
+        late.spread()
+    line.middle()
+    plane.middle()
+    summed = CoreSum(k, "p_")
+    middle = width // 2
+
+    def grad_part(part, which, target):
+        lanes = slice(part * middle, (part + 1) * middle)
+        mixers = jnp.concatenate(
+            [k.b_t[aligned(2 * z + which, shard)] for z in range(4)], 0
+        )
+        k.mixed[...] = dot_nn(mixers, k.v_dy2[:, lanes])
+
+        for z in range(4):
+            at = 2 * z + which
+            mine = jnp.concatenate(
+                [
+                    k.dqkv_t[aligned(at, shard)],
+                    k.dqkv_t[pl.ds(pl.multiple_of(width + at * 2 * shard, 2 * shard), 2 * shard)],
+                ],
+                0,
+            )
+            place_piece(
+                target, part, z, dot_nn(mine, k.v_x1[:, lanes]), k.mixed[z * shard : (z + 1) * shard]
+            )
+
+    for part in BOTH:
+        grad_part(part, 1 - core, k.p_send)
+        summed.start(part)
+    for part in BOTH:
+        grad_part(part, core, k.p_mine)
+    got["mid"].wait()
+    got_proj.wait()
+
+    for i in range(0, width, 256):
+        k.v_mid[:, i : i + 256] += dot_nt(k.dqkv[...], k.v_pooled[i : i + 256])
+    got["xh1"].wait()
+    got["r1"].wait()
+    norm_back(
+        k,
+        rows,
+        lambda at: k.v_mid[at],
+        k.v_xh1,
+        k.v_r1,
+        small_row(k, layer, GAIN),
+        k.v_mid,
+        k.dn,
+        k.sums,
+        0,
+    )
+    k.save(k.v_mid, k.o_low)
+    k.save(k.dn, k.o_dy1)
+    save_sums(k, 2, k.tap_sums)
+    line.spread()
+    plane.finish()
+    k.save(k.x_total, k.o_x)
+    summed.finish()
+    k.save(k.p_mine, k.o_p)
+    if late:
+        late.finish()
+        k.save(k.y_whole, k.o_y)
+    line.finish()
+    k.save(k.z_whole, k.o_z)
+    k.done()
+
+
+def local_back(k, layer, rows, width, final):
+    core = lax.axis_index("seq") % 2
+    sibling, across, up, line_peers, _ = axis_peers()
+    half = LOCAL_WIN // 2
+    pairs, blocks = width // (2 * HD), rows // 128
+    shard = width // 8
+    got = k.load_all(["dy1"])
+    got_mix = k.load(k.w_mix.at[layer], k.v_mix)
+    if final:
+        greet_regroup([sibling, across, up] + line_peers)
+    else:
+        greet([sibling, across, up] + line_peers)
+    plane, line = PlaneSum(k, "x_", k.x_in), LineSum(k, "z_", k.z_in)
+    plane.start()
+    line.start()
+    got.update(k.load_all("q kv".split()))
+    if final:
+        small = SmallSum(k)
+        small.load()
+    for i in range(blocks):
+        k.lbias[i] = local_bias_turned(i, blocks, core == 0, core == 1, 128, half)
+    got["dy1"].wait()
+    got_mix.wait()
+    for i in range(0, width, 256):
+        k.do[:, i : i + 256] = dot_nt(k.v_dy1[...], k.v_mix[i : i + 256]).astype(BF16)
+    got.update(k.load_all("a x low".split()))
+    got_proj = k.load(k.w_local.at[layer], k.v_local)
+    for name in ("q", "kv"):
+        got[name].wait()
+    if final:
+        small.step()
+    k.dkv[...] = jnp.zeros_like(k.dkv)
+    lanes_of = [slice(2 * HD * pair, 2 * HD * (pair + 1)) for pair in range(pairs)]
+    values_of = [slice(width + part.start, width + part.stop) for part in lanes_of]
+
+    def attend_part(i):
+        here, seen = aligned(i, 128), pl.ds(pl.multiple_of(i * 128, 128), 128 + 2 * half)
+        parts = attend_back_blocks(
+            [k.v_q[here, lanes] for lanes in lanes_of],
+            [k.v_kv[seen, lanes] for lanes in lanes_of],
+            [k.v_kv[seen, lanes] for lanes in values_of],
+            [k.do[here, lanes] for lanes in lanes_of],
+            k.lbias[i],
+        )
+        for lanes, values, (grad_q, grad_k, grad_v) in zip(lanes_of, values_of, parts):
+            k.dqkv[here, lanes] = grad_q
+            k.dkv[seen, lanes] += grad_k
+            k.dkv[seen, values] += grad_v
+
+    loop(blocks, attend_part)
+    k.rim_out[...] = k.dkv[pl.ds(pl.multiple_of((rows + half) * (1 - core), half), half)].astype(
+        BF16
+    )
+    rim = k.links.start(k.rim_out, k.rim_got, sibling)
+    got["a"].wait()
+    turn(k.v_a, k.a_t)
+    rim.wait()
+    edge = pl.ds(pl.multiple_of(half + (rows - half) * (1 - core), half), half)
+    k.dkv[edge] += k.rim_got[...].astype(F32)
+    k.dqkv[:, width:] = k.dkv[half : half + rows].astype(BF16)
+    turn(k.dqkv, k.dqkv_t)
+    got["x"].wait()
+    inputs = k.v_x.reshape(rows, width) if len(k.v_x.shape) == 3 else k.v_x
+    summed = CoreSum(k, "l_")
+    middle = width // 2
+
+    def grad_part(part, which, target):
+        lanes = slice(part * middle, (part + 1) * middle)
+        mixers = jnp.concatenate(
+            [k.a_t[aligned(2 * z + which, shard)] for z in range(4)], 0
+        )
+        k.mixed[...] = dot_nn(mixers, k.v_dy1[:, lanes])
+        for z in range(4):
+            mine = k.dqkv_t[aligned(2 * z + which, 3 * shard)]
+            place_piece(
+                target, part, z, dot_nn(mine, inputs[:, lanes]), k.mixed[z * shard : (z + 1) * shard]
+            )
+
+    def residual():
+        got["low"].wait()
+        got_proj.wait()
+        for i in range(0, width, 256):
+            k.v_low[:, i : i + 256] += dot_nt(k.dqkv[...], k.v_local[i : i + 256])
+
+    if not final:
+        for part in BOTH:
+            grad_part(part, 1 - core, k.l_send)
+            summed.start(part)
+        line.middle()
+        plane.middle()
+        for part in BOTH:
+            grad_part(part, core, k.l_mine)
+        residual()
+        k.save(k.v_low, k.o_dx)
+        line.spread()
+        plane.finish()
+        k.save(k.x_total, k.o_x)
+        summed.finish()
+        k.save(k.l_mine, k.o_l)
+        line.finish()
+        k.save(k.z_whole, k.o_z)
+        k.done()
+        return
+    small.step()
+    residual()
+    for i in range(0, rows, 128):
+        k.narrow[i // 128] = k.v_low[i : i + 128].astype(BF16)
+    outward = Regroup(k.loads, k.links, k.narrow, k.regrouped, False)
+    outward.start()
+    line.middle()
+    plane.middle()
+    for part in BOTH:
+        grad_part(part, 1 - core, k.l_send)
+        summed.start(part)
+    small.step()
+    last_plane, last_line = PlaneSum(k, "l_", k.l_mine), LineSum(k, "f_", k.l_total)
+    for part in BOTH:
+        grad_part(part, core, k.l_mine)
+    for part in BOTH:
+        summed.finish(part)
+        last_plane.start(part)
+    plane.finish()
+    before = LineSum(k, "p_", k.x_total)
+    before.start()
+    small.step()
+    line.spread()
+    last_plane.middle(0)
+    last_plane.middle(1)
+    line.finish()
+    k.save(k.z_whole, k.o_z)
+    before.middle()
+    for part in BOTH:
+        last_plane.finish(part)
+        last_line.start(part)
+    small.finish()
+    before.spread()
+    outward.wait()
+    k.save(k.regrouped, k.o_dx)
+    last_line.middle(0)
+    before.finish()
+    k.save(k.p_whole, k.o_p)
+    last_line.middle(1)
+    last_line.spread(0)
+    last_line.spread(1)
+    last_line.finish()
+    k.save(k.f_whole, k.o_f)
+    k.done()
+
+
+class SmallSum:
+    def __init__(self, k):
+        self.k = k
+        sibling, across, up, line, _ = axis_peers()
+        self.order = [[sibling], [across], [up], line]
+        self.at, self.slot = 0, 0
+
+    def load(self):
+        k = self.k
+        self.copies = []
+        for i in range(k.s_sum.shape[0]):
+            for source, first, last in ((k.s_feed[i], 0, 8), (k.s_pool[i], 8, 24)):
+                self.copies.append(k.load(source, k.s_sum.at[i, first:last]))
+
+    def step(self):
+        k = self.k
+        for copy in self.copies:
+            copy.wait()
+        if self.at > 0:
+            for _ in self.copies:
+                k.s_sum[...] += k.s_got[self.slot]
+                self.slot += 1
+        if self.at < len(self.order):
+            self.copies = [
+                k.links.start(k.s_sum, k.s_got.at[self.slot + i], device)
+                for i, device in enumerate(self.order[self.at])
+            ]
+        self.at += 1
+
+    def finish(self):
+        self.step()
+        self.k.save(self.k.s_sum, self.k.o_small)
+
+
+def save_sums(k, count, taps=None):
+    for i in range(count):
+        k.row_sums[i : i + 1] = jnp.sum(k.sums[i], 0, keepdims=True)
+    at = count
+    if taps is not None:
+        for side in range(2):
+            for t in range(5):
+                k.row_sums[at : at + 1] = jnp.sum(
+                    taps[side, 8 * t : 8 * t + 8], 0, keepdims=True
+                )
+                at += 1
+    k.row_sums[at:] = jnp.zeros((k.row_sums.shape[0] - at, k.row_sums.shape[1]), F32)
+    k.save(k.row_sums, k.o_sums)
+
+
+def block_of(width):
+    return (width // 16, width // 2)
+
+
+def group_shape(block):
+    return (2, 4, 2, 2, 2) + block
+
+
+def total_shape(block):
+    return (2, 4, 2) + block
+
+
+def whole_shape(block):
+    return (2, 2, 2, 2) + block
+
+
+def feed_back_call(layer, last, dy, small, kept, w_down, w_up, x_in, z_in, outputs):
+    rows, width = kept.o_xh3.shape
+    ff = kept.o_g.shape[1]
+    block = block_of(width)
+    full, wide = (rows, width), vmem((rows, width))
+    s = Scratch()
+    args = dict(small_in=(small, ANY), w_down=(w_down, ANY), w_up=(w_up, ANY))
+    s.bring(args, dy=dy, xh3=kept.o_xh3, r3=kept.o_r3, g=kept.o_g, gp=kept.o_gp)
+    s.bring(args, x2=kept.o_x2, xh2=kept.o_xh2, r2=kept.o_r2)
+    outs = dict(o_mid=(full, F32), o_dy2=(full, BF16), o_sums=((8, width), F32))
+    outs.update(o_r=(total_shape(block), BF16), o_e=(group_shape(block), BF16))
+    s.add(small=vmem(small.shape, F32), sums=vmem((4, 8, width), F32))
+    s.add(v_down=vmem(w_down.shape[1:]), v_up=vmem(w_up.shape[1:]))
+    s.add(row_sums=vmem((8, width), F32), res=vmem(full, F32), dn=wide, dn2=wide)
+    s.add(dn_t=vmem((width, rows)), x2_t=vmem((width, rows)), du=vmem((rows, ff)))
+    s.core("r_", block)
+    s.core("e_", block)
+    s.plane("r_", block)
+    if last:
+        by_doc = (4, rows // 4, width)
+        args.update(x3=(outputs.reshape(by_doc), ANY))
+        outs.update(o_out=(by_doc, BF16))
+        s.add(regrouped=vmem(by_doc))
+    else:
+        args.update(x_in=(x_in, ANY), z_in=(z_in, ANY))
+        outs.update(o_y=((2, 2) + block, BF16), o_z=(whole_shape(block), BF16))
+        s.plane("x_", block)
+        s.line("y_", block)
+        s.line("z_", block)
+    s.sems(40, 16, 48)
+    return run_kernel(
+        lambda k: feed_back(k, layer, rows, width, ff, last),
+        "feed_back_%d" % layer,
+        2 + layer,
+        args,
+        outs,
+        s,
+    )
+
+
+def pooled_back_call(layer, mid, dy2, small, pbias, kept, w_mix2, w_pooled, x_in, z_in, y_in):
+    rows, width = mid.shape
+    pool = rows // 4
+    block = block_of(width)
+    full, wide = (rows, width), vmem((rows, width))
+    s = Scratch()
+    args = dict(small_in=(small, ANY), w_mix2=(w_mix2, ANY), w_pooled=(w_pooled, ANY))
+    args.update(x_in=(x_in, ANY), z_in=(z_in, ANY))
+    s.bring(args, mid=mid, dy2=dy2, b=kept.o_b, q2=kept.o_q2, kv2=kept.o_kv2, pk=kept.o_pk)
+    s.bring(args, x1=kept.o_x1, xh1=kept.o_xh1, r1=kept.o_r1, pbias=pbias)
+    outs = dict(o_low=(full, F32), o_dy1=(full, BF16), o_sums=((16, width), F32))
+    outs.update(o_p=(group_shape(block), BF16), o_x=(total_shape(block), BF16))
+    outs.update(o_z=(whole_shape(block), BF16))
+    s.add(small=vmem(small.shape, F32), v_mix2=vmem(w_mix2.shape[1:]))
+    s.add(v_pooled=vmem(w_pooled.shape[1:]), sums=vmem((2, 8, width), F32))
+    s.add(row_sums=vmem((16, width), F32), tap_sums=vmem((2, 40, width), F32), do=wide, dn=wide)
+    rim, turned = vmem((pool + 16, 2 * width)), vmem((width, rows))
+    s.add(dkv=vmem((2 * pool, 2 * width), F32), rim_out=rim, rim_got=rim)
+    s.add(total=vmem((pool + 8, 2 * width), F32), kvf=vmem((2 * width // 128, rows, 128), F32))
+    s.add(dqkv=vmem((rows, 3 * width)), dqkv_t=vmem((3 * width, rows)), b_t=turned)
+    s.add(mixed=vmem((width // 2, width // 2), F32))
+    s.core("p_", block)
+    s.plane("x_", block)
+    s.line("z_", block)
+    if y_in is not None:
+        args.update(y_in=(y_in, ANY))
+        outs.update(o_y=(whole_shape(block), BF16))
+        s.add(y_whole=vmem(whole_shape(block)))
+    s.sems(40, 16, 48)
+    return run_kernel(
+        lambda k: pooled_back(k, layer, rows, width),
+        "pooled_back_%d" % layer,
+        4 + layer,
+        args,
+        outs,
+        s,
+    )
+
+
+def local_back_call(layer, final, low, dy1, kept, w_mix, w_local, x_in, z_in, sums):
+    rows, width = low.shape
+    half = LOCAL_WIN // 2
+    block = block_of(width)
+    s = Scratch()
+    args = dict(w_mix=(w_mix, ANY), w_local=(w_local, ANY), x_in=(x_in, ANY), z_in=(z_in, ANY))
+    s.bring(args, low=low, dy1=dy1, a=kept.o_a, q=kept.o_q, kv=kept.o_kv, x=kept.o_x)
+    outs = dict(o_z=(whole_shape(block), BF16))
+    by_doc, total = (4, rows // 4, width), (len(sums), 24, width)
+    if final:
+        whole = (whole_shape(block), BF16)
+        for i, (feed, pooled) in enumerate(sums):
+            args["s_feed%d" % i], args["s_pool%d" % i] = (feed, ANY), (pooled, ANY)
+        outs.update(o_dx=(by_doc, BF16), o_p=whole, o_f=whole, o_small=(total, F32))
+    else:
+        outs.update(o_dx=((rows, width), F32), o_l=(group_shape(block), BF16))
+        outs.update(o_x=(total_shape(block), BF16))
+    s.add(v_mix=vmem(w_mix.shape[1:]), v_local=vmem(w_local.shape[1:]))
+    s.add(lbias=vmem((rows // 128, 128 + 2 * half, 128), F32), do=vmem((rows, width)))
+    s.add(dkv=vmem((rows + 2 * half, 2 * width), F32))
+    s.add(rim_out=vmem((half, 2 * width)), rim_got=vmem((half, 2 * width)))
+    s.add(dqkv=vmem((rows, 3 * width)), dqkv_t=vmem((3 * width, rows)))
+    s.add(a_t=vmem((width, rows)), mixed=vmem((width // 2, width // 2), F32))
+    s.core("l_", block)
+    s.plane("x_", block)
+    s.line("z_", block)
+    if final:
+        s.add(narrow=vmem(by_doc), regrouped=vmem(by_doc))
+        s.add(s_sum=vmem(total, F32), s_got=vmem((6,) + total, F32))
+        s.plane("l_", block)
+        s.line("p_", block)
+        s.line("f_", block)
+    s.sems(48, 16, 72)
+
+    def body(k):
+        if final:
+            k.s_feed = [getattr(k, "s_feed%d" % i) for i in range(len(sums))]
+            k.s_pool = [getattr(k, "s_pool%d" % i) for i in range(len(sums))]
+        local_back(k, layer, rows, width, final)
+
+    return run_kernel(
+        body,
+        "local_back_%d" % layer,
+        6 + layer,
+        args,
+        outs,
+        s,
+    )
+
+
+def by_chip(
+    inputs,
+    question_count,
+    question_at,
+    local_proj,
+    local_mixer,
+    pooled_proj,
+    pool_taps,
+    pooled_mixer,
+    expand_weight,
+    reduce_weight,
+    norm_gain,
+    norm_shift,
+    output_grad,
+):
+    docs_here, tok_here, width = inputs.shape
+    layers, ff = local_proj.shape[0], expand_weight.shape[2]
+    small = jnp.concatenate([norm_gain, norm_shift, pool_taps.reshape(layers, 10, width)], 1)
+    weights = (local_proj, local_mixer, pooled_proj, pooled_mixer, expand_weight, reduce_weight)
+    hidden, kept, bias = inputs, [], None
+    for layer in range(layers):
+        first, last = layer == 0, layer == layers - 1
+        extra = (question_count, question_at, output_grad) if first else bias
+        made = forward_call(layer, first, last, hidden, small, weights, extra)
+        if first:
+            grad, bias, bias_t = made.o_grad, made.o_pbias, made.o_pbias_t
+        kept.append(made)
+        hidden = made.o_out
+    x_in = z_in = None
+    reduced, expanded, pooled_sums, local_sums, sums = {}, {}, {}, {}, []
+    for layer in reversed(range(layers)):
+        last = layer == layers - 1
+        saved = kept[layer]
+        fed = feed_back_call(
+            layer, last, grad, small, saved, reduce_weight, expand_weight, x_in, z_in, hidden
+        )
+        if last:
+            outputs = fed.o_out
+        else:
+            pooled_sums[layer + 1] = fed.o_z
+        pooled = pooled_back_call(
+            layer,
+            fed.o_mid,
+            fed.o_dy2,
+            small,
+            bias_t,
+            saved,
+            pooled_mixer,
+            pooled_proj,
+            fed.o_e,
+            fed.o_r,
+            None if last else fed.o_y,
+        )
+        reduced[layer] = pooled.o_z
+        if not last:
+            local_sums[layer + 1] = pooled.o_y
+        sums.insert(0, (fed.o_sums, pooled.o_sums))
+        local = local_back_call(
+            layer,
+            layer == 0,
+            pooled.o_low,
+            pooled.o_dy1,
+            saved,
+            local_mixer,
+            local_proj,
+            pooled.o_p,
+            pooled.o_x,
+            sums,
+        )
+        expanded[layer] = local.o_z
+        if layer > 0:
+            grad, x_in, z_in = local.o_dx, local.o_l, local.o_x
+    pooled_sums[0], local_sums[0] = local.o_p, local.o_f
+    groups = [[group[i] for i in range(layers)] for group in (reduced, expanded, local_sums, pooled_sums)]
+    return finish_call(outputs, local.o_dx, local.o_small, groups, layers, width, ff)
+
+
+def finish(k, layers, width, ff):
+    part, feed = width // 8, ff // 8
+    me = lax.axis_index("seq")
+    order = list(reversed(range(layers)))
+    names = ["g%d" % i for i in range(4 * layers)]
+    got = [k.load(getattr(k, name), getattr(k, "v_" + name)) for name in names]
+    got_dx, got_small = k.load(k.dx, k.v_dx), k.load(k.small_sum, k.v_small_sum)
+    got_out = k.load(k.outputs, k.v_outputs)
+
+    def whole(group, layer, axis):
+        got[group * layers + layer].wait()
+        block = getattr(k, "v_" + names[group * layers + layer])
+        parts = [block[i].reshape(-1, block.shape[-1]).astype(F32) for i in BOTH]
+        return jnp.concatenate(parts, axis)
+
+    def put(layer, source, target, value):
+        source[layer] = value
+        k.save(source.at[layer], target.at[layer])
+
+    for layer in order:
+        put(layer, k.v_down, k.o_down, whole(0, layer, 0).T)
+        put(layer, k.v_up, k.o_up, whole(1, layer, 0))
+    got_out.wait()
+    k.save(k.v_outputs, k.o_outputs)
+    got_dx.wait()
+    for i in range(4):
+        k.v_dx32[i] = k.v_dx[i].astype(F32)
+    k.save(k.v_dx32, k.o_dx)
+    for layer in order:
+        local = whole(2, layer, 1)
+        put(layer, k.v_local, k.o_local, local[: 3 * part])
+        put(layer, k.v_mix, k.o_mix, local[3 * part :])
+        pooled = whole(3, layer, 1)
+        put(layer, k.v_query, k.o_query, pooled[:part])
+        put(layer, k.v_kv, k.o_kv, pooled[part : 3 * part])
+        put(layer, k.v_mix2, k.o_mix2, pooled[3 * part :])
+    got_small.wait()
+    small = k.v_small_sum[...]
+    mine = jnp.zeros(small.shape[:2] + (part,), F32)
+    for i in range(8):
+        mine = jnp.where(me == i, small[:, :, i * part : (i + 1) * part], mine)
+    for layer in range(layers):
+        rows = mine[layer]
+        for i, (gain, shift) in enumerate(((8, 9), (2, 3), (0, 1))):
+            k.v_gain[i, layer : layer + 1] = rows[gain : gain + 1]
+            k.v_shift[i, layer : layer + 1] = rows[shift : shift + 1]
+        for side in range(2):
+            for t in range(5):
+                at = 10 + 5 * side + t
+                k.v_taps[layer, t, side : side + 1] = rows[at : at + 1]
+    k.save(k.v_gain, k.o_gain)
+    k.save(k.v_shift, k.o_shift)
+    k.save(k.v_taps, k.o_taps)
+    k.done()
+
+
+def finish_call(outputs, dx, small_sum, groups, layers, width, ff):
+    part, feed = width // 8, ff // 8
+    args = {}
+    s = Scratch()
+    s.bring(args, outputs=outputs, dx=dx, small_sum=small_sum)
+    s.add(v_dx32=vmem(dx.shape, F32))
+    for i, array in enumerate(array for group in groups for array in group):
+        s.bring(args, **{"g%d" % i: array})
+    mixer, few = (layers, part, width), (3, layers, part)
+    shapes = dict(local=(layers, 3 * part, width), mix=mixer, query=mixer)
+    shapes.update(kv=(layers, 2 * part, width), taps=(layers, 5, 2, part), mix2=mixer)
+    shapes.update(up=(layers, width, feed), down=(layers, feed, width), gain=few, shift=few)
+    outs = dict(o_outputs=(outputs.shape, BF16), o_dx=(dx.shape, F32))
+    for name, shape in shapes.items():
+        outs["o_" + name] = (shape, F32)
+        s.add("v_", **{name: vmem(shape, F32)})
+    s.sems(16, 32, 1)
+    made = run_kernel(lambda k: finish(k, layers, width, ff), "finish", None, args, outs, s)
+    made.o_local, made.o_query, made.o_kv = (
+        jnp.swapaxes(array, 1, 2) for array in (made.o_local, made.o_query, made.o_kv)
+    )
+    made.o_taps = jnp.swapaxes(made.o_taps, 1, 2)
+    made.o_gain, made.o_shift = jnp.swapaxes(made.o_gain, 0, 1), jnp.swapaxes(made.o_shift, 0, 1)
+    return tuple(vars(made).values())
 
 
 def with_halo(array, sides, width):
@@ -126,7 +1724,7 @@
     return (grad_ext, jnp.stack(tap_grads, 1))
 
 
-def per_device(
+def by_sequence(
     inputs,
     question_count,
     question_at,
@@ -213,25 +1811,25 @@
             hidden_now.shape
         )
         result = layer_norm(third_sum, norm_gain[layer_at, 2], norm_shift[layer_at, 2])
-        forward_saved = {
-            "in_rows": in_rows,
-            "local_heads": local_heads,
-            "near_kv": forward_near_kv,
-            "local_lse": local_lse,
-            "local_mix": local_mix,
-            "first_sum": first_sum,
-            "second_in": second_in,
-            "pooled_heads": pooled_heads,
-            "extended": extended,
-            "saved_pool": forward_all_pooled,
-            "pooled_lse": pooled_lse,
-            "pooled_mix": pooled_mix,
-            "second_sum": second_sum,
-            "ffn_in": ffn_in,
-            "up_proj": up_proj,
-            "activated": activated,
-            "third_sum": third_sum,
-        }
+        forward_saved = SimpleNamespace(
+            in_rows=in_rows,
+            local_heads=local_heads,
+            near_kv=forward_near_kv,
+            local_lse=local_lse,
+            local_mix=local_mix,
+            first_sum=first_sum,
+            second_in=second_in,
+            pooled_heads=pooled_heads,
+            extended=extended,
+            saved_pool=forward_all_pooled,
+            pooled_lse=pooled_lse,
+            pooled_mix=pooled_mix,
+            second_sum=second_sum,
+            ffn_in=ffn_in,
+            up_proj=up_proj,
+            activated=activated,
+            third_sum=third_sum,
+        )
         hidden_now = result
         saved_all.append(forward_saved)
     outputs = hidden_now.astype(jnp.bfloat16)
@@ -243,34 +1841,34 @@
         bias_row = norm_shift[layer_at]
         taps = pool_taps[layer_at].reshape(2, 5, heads, HD)
         unused_third, pull_third = jax.vjp(
-            layer_norm, backward_saved["third_sum"], gain_row[2], bias_row[2]
+            layer_norm, backward_saved.third_sum, gain_row[2], bias_row[2]
         )
         grad_third, gain_third, bias_third = pull_third(grad_now)
         grad_down_in = as_rows(grad_third.astype(jnp.bfloat16))
-        down_grad = mul_first(backward_saved["activated"], grad_down_in)
+        down_grad = mul_first(backward_saved.activated, grad_down_in)
         grad_act = mul_last(grad_down_in, reduce_weight[layer_at])
-        unused_gelu, pull_gelu = jax.vjp(exact_gelu, backward_saved["up_proj"])
+        unused_gelu, pull_gelu = jax.vjp(exact_gelu, backward_saved.up_proj)
         grad_up = pull_gelu(grad_act)[0].astype(jnp.bfloat16)
-        up_grad = mul_first(as_rows(backward_saved["ffn_in"]), grad_up)
+        up_grad = mul_first(as_rows(backward_saved.ffn_in), grad_up)
         grad_second = grad_third + mul_last(grad_up, expand_weight[layer_at]).reshape(
             grad_now.shape
         )
         unused_second, pull_second = jax.vjp(
-            layer_norm, backward_saved["second_sum"], gain_row[1], bias_row[1]
+            layer_norm, backward_saved.second_sum, gain_row[1], bias_row[1]
         )
         grad_mid, gain_second, bias_second = pull_second(grad_second)
         grad_pool_mix = as_rows(grad_mid.astype(jnp.bfloat16))
-        out2_grad = mul_first(as_rows(backward_saved["pooled_mix"]), grad_pool_mix)
+        out2_grad = mul_first(as_rows(backward_saved.pooled_mix), grad_pool_mix)
         grad_pool_out = (
             mul_last(grad_pool_mix, pooled_mixer[layer_at]).astype(jnp.bfloat16).reshape(head_shape)
         )
-        all_pooled = backward_saved["saved_pool"]
+        all_pooled = backward_saved.saved_pool
         grad_pool_query, grad_pool_key, grad_pool_value = attend_back(
-            backward_saved["pooled_heads"][:, :, 0],
+            backward_saved.pooled_heads[:, :, 0],
             all_pooled[:, :, 0],
             all_pooled[:, :, 1],
             pool_allowed,
-            backward_saved["pooled_lse"],
+            backward_saved.pooled_lse,
             grad_pool_out,
         )
         own_key = lax.psum_scatter(
@@ -280,7 +1878,7 @@
             grad_pool_value.astype(jnp.bfloat16), "seq", scatter_dimension=1, tiled=True
         ).astype(jnp.float32)
         grad_ext, taps_grad = taps_back(
-            backward_saved["extended"], taps, jnp.stack([own_key, own_value], 2)
+            backward_saved.extended, taps, jnp.stack([own_key, own_value], 2)
         )
         from_next = from_behind(grad_ext[:, :2].astype(jnp.bfloat16), "seq", -1).astype(jnp.float32)
         grad_kv_second = grad_ext[:, 2:].at[:, tok_here - 2 :].add(from_next)
@@ -289,26 +1887,26 @@
             .astype(jnp.bfloat16)
             .reshape(-1, 3 * width)
         )
-        proj2_grad = mul_first(as_rows(backward_saved["second_in"]), grad_heads_two)
+        proj2_grad = mul_first(as_rows(backward_saved.second_in), grad_heads_two)
         grad_first = grad_mid + mul_last(grad_heads_two, pooled_proj[layer_at]).reshape(
             grad_now.shape
         )
         unused_first, pull_first = jax.vjp(
-            layer_norm, backward_saved["first_sum"], gain_row[0], bias_row[0]
+            layer_norm, backward_saved.first_sum, gain_row[0], bias_row[0]
         )
         grad_low, gain_first, bias_first = pull_first(grad_first)
         grad_local_mix = as_rows(grad_low.astype(jnp.bfloat16))
-        out1_grad = mul_first(as_rows(backward_saved["local_mix"]), grad_local_mix)
+        out1_grad = mul_first(as_rows(backward_saved.local_mix), grad_local_mix)
         grad_local_out = (
             mul_last(grad_local_mix, local_mixer[layer_at]).astype(jnp.bfloat16).reshape(head_shape)
         )
-        near_kv = backward_saved["near_kv"]
+        near_kv = backward_saved.near_kv
         grad_local_query, grad_near_key, grad_near_value = attend_back(
-            backward_saved["local_heads"][:, :, 0],
+            backward_saved.local_heads[:, :, 0],
             near_kv[:, :, 0],
             near_kv[:, :, 1],
             local_allowed,
-            backward_saved["local_lse"],
+            backward_saved.local_lse,
             grad_local_out,
         )
         grad_near = jnp.stack([grad_near_key, grad_near_value], 2)
@@ -326,7 +1924,7 @@
             .astype(jnp.bfloat16)
             .reshape(-1, 3 * width)
         )
-        proj1_grad = mul_first(as_rows(backward_saved["in_rows"]), grad_heads_one)
+        proj1_grad = mul_first(as_rows(backward_saved.in_rows), grad_heads_one)
         grad_bottom = grad_low + mul_last(grad_heads_one, local_proj[layer_at]).reshape(
             grad_now.shape
         )
@@ -406,6 +2004,13 @@
 
 
 def solution(mesh):
+    planes, places = mesh.shape["doc"], mesh.shape["seq"]
+
+    def per_device(inputs, *others):
+        docs_here, tok_here, _ = inputs.shape
+        whole = docs_here == 4 and 2 * docs_here == places and planes == 4 and tok_here == 128
+        return (by_chip if whole else by_sequence)(inputs, *others)
+
     return jax.shard_map(
         per_device,
         mesh=mesh,

time: 2540 us -> 354 us (0.14); the launches traced: 2500 us -> 349 us
  local copies, waits for them, and re-layouts: 1050 us -> 2.33 us
  waiting for transfers between devices: 863 us -> 0 us
  Pallas kernels: 0 us -> 345 us
  other arithmetic: 281 us -> 0.67 us
  matrix products: 216 us -> 0 us
  starting transfers between devices: 60.3 us -> 0 us
    slice x36 -> x0, local copies, waits for them, and re-layouts: 586 us -> none  [the longest x8 428 us: apply_taps(): extended[:, tap_at:tap_at + 4 * pool_rows:4] * taps[:, tap_at]]
    unnamed x21 -> x0, waiting for transfers between devices: 385 us -> none
    pallas_call x0 -> x9, Pallas kernels: none -> 345 us  [run_kernel(): pl.pallas_call(kernel, out_shape=[jax.ShapeDtypeStruct(shape, kind) for s...]
    reduce_scatter x4 -> x0, waiting for transfers between devices: 248 us -> none  [the longest x1 100 us: per_device(): lax.psum_scatter(stacked[7].astype(jnp.bfloat16), 'seq', scatter_dimensio...]
    dot_general x60 -> x0, matrix products: 216 us -> none  [the longest x12 59.7 us: mul_plain(): return jnp.dot(left_rows, right_mat, preferred_element_type=jnp.float32)]
    scatter-add x4 -> x0, local copies, waits for them, and re-layouts: 140 us -> none  [the longest x2 78.6 us: per_device(): grad_kv_first.at[:, tok_here - half_win:].add(came_back[:, 3 * half_win:])]
    unnamed x545 -> x3, local copies, waits for them, and re-layouts: 130 us -> 2.32 us
    all_gather x2 -> x0, waiting for transfers between devices: 127 us -> none  [per_device(): forward_all_pooled = lax.all_gather(pooled, 'seq', axis=1, tiled=True)]
  transfers between devices with their start and end apart: 26 -> 0, of which waited for: 17 -> 0; matrix products, arithmetic and copies ran while one was open for 12% -> 0% of each run, Pallas kernels for 0% -> 0%
where the time goes in v1:
time: 354 us; the launch traced here: 349 us
  Pallas kernels  345 us (97%)
    pallas_call x9, Pallas kernels, run_kernel(): pl.pallas_call(kernel, out_shape=[jax.ShapeDtypeStruct(shape, kind) for s...  345 us

profile of v1, /device:TPU:0, one launch (start us, length us, event | category | flops | bytes accessed | tf_op | source)
XLA Modules:
  0.0 348.5 jit_solution(7746526436571775659)
XLA Ops:
  0.6 0.7 copy.29
  1.4 0.7 copy.30
  2.1 0.9 copy.28
  3.0 0.7 pad_maximum_fusion.refs_1_.refs_0_
  3.7 46.6 %forward_0.1 = (bf16[4,128,768]{2,1,0:T(8,128)(2,1)}, bf16[512,768]{1,0:T(8,128)(2,1)}, bf16[640,1536]{1,0:T(8,128)(2,1)}, bf16[512,768]{1,0:T(8,128)(2,1)}, bf1...) custom-call(bf16[4,128,768]{2,1,0:T(8,128)(2,1)} %refs_0_.3, ...), custom_call_target="tpu_custom_call" | custom-call | tf_op jit(solution)/shard_map/forward_0/pallas_call | solution.py:308
  50.3 28.8 %forward_1.1 = (bf16[512,768]{1,0:T(8,128)(2,1)}, bf16[512,768]{1,0:T(8,128)(2,1)}, bf16[640,1536]{1,0:T(8,128)(2,1)}, bf16[512,768]{1,0:T(8,128)(2,1)}, bf16[51...) custom-call(f32[512,768]{1,0:T(8,128)} %get-tuple-element.101.refs_0, ...), custom_call_target="tpu_custom_call" | custom-call | tf_op jit(solution)/shard_map/forward_1/pallas_call | solution.py:308
  79.1 38.0 %feed_back_1.1 = (f32[512,768]{1,0:T(8,128)}, bf16[512,768]{1,0:T(8,128)(2,1)}, f32[8,768]{1,0:T(8,128)}, bf16[2,4,2,48,384]{4,3,2,1,0:T(8,128)(2,1)}, bf16[2,4,...) custom-call(f32[2,16,768]{2,1,0:T(8,128)} %pad_maximum_fusion.refs_1_.refs_0_, ...), custom_call_target="tpu_custom_call" | custom-call | tf_op jit(solution)/shard_map/feed_back_1/pallas_call | solution.py:308
  117.1 29.2 %pooled_back_1.1 = (f32[512,768]{1,0:T(8,128)}, bf16[512,768]{1,0:T(8,128)(2,1)}, f32[16,768]{1,0:T(8,128)}, bf16[2,4,2,2,2,48,384]{6,5,4,3,2,1,0:T(8,128)(2,1)}...) custom-call(f32[2,16,768]{2,1,0:T(8,128)} %pad_maximum_fusion.refs_1_.refs_0_, ...), custom_call_target="tpu_custom_call" | custom-call | tf_op jit(solution)/shard_map/pooled_back_1/pallas_call | solution.py:308
  146.2 31.7 %local_back_1.1 = (bf16[2,2,2,2,48,384]{5,4,3,2,1,0:T(8,128)(2,1)}, f32[512,768]{1,0:T(8,128)}, bf16[2,4,2,2,2,48,384]{6,5,4,3,2,1,0:T(8,128)(2,1)}, bf16[2,4,2,48,384]{4,3,2,1,0:T(8,128)(2,1)}) custom-call(bf16[2,768,768]{2,1,0:T(8,128)(2,1)} %refs_0_.5, bf16[2,768,2304]{2,1,0:T(8,128)(2,1)} %refs_1_.11, ...), custom_call_target="tpu_custom_call" | custom-call | tf_op jit(solution)/shard_map/local_back_1/pallas_call | solution.py:308
  178.0 47.8 %feed_back_0.1 = (f32[512,768]{1,0:T(8,128)}, bf16[512,768]{1,0:T(8,128)(2,1)}, f32[8,768]{1,0:T(8,128)}, bf16[2,4,2,48,384]{4,3,2,1,0:T(8,128)(2,1)}, bf16[2,4,...) custom-call(f32[2,16,768]{2,1,0:T(8,128)} %pad_maximum_fusion.refs_1_.re, ...), custom_call_target="tpu_custom_call" | custom-call | tf_op jit(solution)/shard_map/feed_back_0/pallas_call | solution.py:308
  225.8 33.8 %pooled_back_0.1 = (f32[512,768]{1,0:T(8,128)}, bf16[512,768]{1,0:T(8,128)(2,1)}, f32[16,768]{1,0:T(8,128)}, bf16[2,4,2,2,2,48,384]{6,5,4,3,2,1,0:T(8,128)(2,1)}...) custom-call(f32[2,16,768]{2,1,0:T(8,128)} %pad_maximum_fusion.refs_1, ...), custom_call_target="tpu_custom_call" | custom-call | tf_op jit(solution)/shard_map/pooled_back_0/pallas_call | solution.py:308
  259.6 81.4 %local_back_0.1 = (bf16[2,2,2,2,48,384]{5,4,3,2,1,0:T(8,128)(2,1)}, bf16[4,128,768]{2,1,0:T(8,128)(2,1)}, bf16[2,2,2,2,48,384]{5,4,3,2,1,0:T(8,128)(2,1)}, bf16[...) custom-call(bf16[2,768,768]{2,1,0:T(8,128)(2,1)} %refs_0_.5, bf16[2,768,2304]{2,1,0:T(8,128)(2,1)} %refs_1_.11, ...), custom_call_target="tpu_custom_call" | custom-call | tf_op jit(solution)/shard_map/local_back_0/pallas_call | solution.py:308
  341.0 7.2 %finish.1 = (bf16[4,128,768]{2,1,0:T(8,128)(2,1)}, f32[4,128,768]{2,1,0:T(8,128)}, f32[2,288,768]{2,1,0:T(8,128)}, f32[2,96,768]{2,1,0:T(8,128)}, f32[2,96,768]{...) custom-call(bf16[4,128,768]{2,1,0:T(8,128)(2,1)} %get-tuple-element., ...), custom_call_target="tpu_custom_call" | custom-call | tf_op jit(solution)/shard_map/finish/pallas_call | solution.py:308
  (1 shorter events, 0.0 us)

commit v2 on v1

--- a/solution.py
+++ b/solution.py
@@ -226,16 +226,15 @@
 
 
 def gelu_rows(u):
-    z = jnp.abs(u) * (0.5**0.5)
-    t = 1.0 / (1.0 + 0.3275911 * z)
-    series = 1.061405429 * t - 1.453152027
-    series = series * t + 1.421413741
-    series = series * t - 0.284496736
-    series = series * t + 0.254829592
-    bell = jnp.exp(-(z * z))
-    tail = 0.5 * series * t * bell
+    t = 1.0 / (1.0 + (0.3275911 * 0.5**0.5) * jnp.abs(u))
+    series = 0.5307027145 * t - 0.7265760135
+    series = series * t + 0.7107068705
+    series = series * t - 0.142248368
+    series = series * t + 0.127414796
+    bell = jnp.exp2((u * u) * -0.7213475204444817)
+    tail = series * t * bell
     share = jnp.where(u < 0, tail, 1.0 - tail)
-    return u * share, share + u * bell * 0.3989422804014327
+    return u * share, share + (u * 0.3989422804014327) * bell
 
 
 def vmem(shape, kind=BF16):
@@ -258,7 +257,7 @@
 
     def line(self, tag, block):
         whole = vmem((2, 2, 2, 2) + block)
-        self.add(tag, own=vmem((2, 2) + block), got=vmem((2, 3, 2) + block), whole=whole)
+        self.add(tag, own=vmem((2, 2) + block), got=vmem((2, 4, 2) + block), whole=whole)
 
     def core(self, tag, block):
         group = vmem((2, 4, 2, 2, 2) + block)
@@ -303,7 +302,10 @@
     names = list(args) + list(outs) + scratch.names
 
     def kernel(*refs):
-        body(Kernel(names, refs))
+        k = Kernel(names, refs)
+        body(k)
+        for used, sems in ((k.loads, k.load_sems), (k.saves, k.save_sems), (k.links, k.send_sems)):
+            assert used.used <= sems.shape[0]
 
     made = pl.pallas_call(
         kernel,
@@ -569,7 +571,7 @@
     s.add(xf=full, x1f=full, acc=full, rt=rate, rt2=rate, rt3=rate, g=feed, gp=feed)
     part, pooled = vmem((rows, 512), F32), vmem((pool, 2 * width))
     s.add(up_a=part, up_b=part, kv=vmem(*kv), kv2=vmem((rows, 2 * width)))
-    s.add(kvf=vmem((2 * width // 128, rows + 8, 128), F32), pk=vmem((2 * pool, 2 * width)))
+    s.add(kvf=vmem((2 * width // 128, rows + 16, 128), F32), pk=vmem((2 * pool, 2 * width)))
     aux = vmem((16, 2 * width), F32)
     s.add(halo=vmem((half, 2 * width)), kp_own=pooled, kp_got=pooled, aux_own=aux, aux_got=aux)
     s.add(lbias=vmem((rows // 128, 128, 128 + 2 * half), F32))
@@ -755,6 +757,78 @@
         for part in parts or BOTH:
             for copy in self.copy[part]:
                 copy.wait()
+
+
+class RelaySum(LineSum):
+    def __init__(self, k, tag, source):
+        super().__init__(k, tag, source)
+        self.doc, me = lax.axis_index("doc"), lax.axis_index("seq")
+        self.core, self.z = me % 2, me // 2
+        self.near = self.z + 1 - 2 * (self.z % 2)
+        self.far = [2 - 2 * (self.z // 2) + i for i in range(2)]
+        self.inner = (self.z == 1) | (self.z == 2)
+        self.first = {}
+
+    def _send(self, part, source, slot, send, recv, z):
+        at = self.first[part]
+        return pltpu.make_async_remote_copy(
+            src_ref=source,
+            dst_ref=self.got.at[part, slot],
+            send_sem=self.links.send.at[at + send],
+            recv_sem=self.links.recv.at[at + recv],
+            device_id=(self.doc, 2 * z + self.core),
+            device_id_type=MESH,
+        )
+
+    def _beside(self, part):
+        return self._send(part, self.source.at[part, self.near], 0, 0, 0, self.near)
+
+    def _past(self, part, i):
+        return self._send(part, self.source.at[part, self.far[i]], 2 + i, 1 + i, 1 + i, self.near)
+
+    def _across(self, part, i):
+        return self._send(part, self.got.at[part, 2 + i], 1, 3 + i, 3, self.far[i])
+
+    def start(self, *parts):
+        for part in parts or BOTH:
+            self.first[part] = self.links.used
+            self.links.used += 5
+
+            @pl.when(jnp.logical_not(self.inner))
+            def _():
+                for i in range(2):
+                    self._past(part, i).start()
+
+            self._beside(part).start()
+
+    def relay(self, part):
+        @pl.when(self.inner)
+        def _():
+            for i in range(2):
+                self._past(part, i).wait_recv()
+                self.got[part, 2 + i] += self.source[part, self.far[i]]
+                self._across(part, i).start()
+
+    def settle(self, *parts):
+        for part in parts or BOTH:
+            self._beside(part).wait()
+            self._across(part, 0).wait_recv()
+
+            @pl.when(self.inner)
+            def _():
+                for i in range(2):
+                    self._across(part, i).wait_send()
+
+            @pl.when(jnp.logical_not(self.inner))
+            def _():
+                for i in range(2):
+                    self._past(part, i).wait_send()
+
+            for half in range(2):
+                total = self.source[part, self.z, half].astype(F32)
+                for i in range(2):
+                    total = total + self.got[part, i, half].astype(F32)
+                self.whole[part, half, self.y, self.x] = total.astype(BF16)
 
 
 def norm_back(k, rows, incoming, plain_ref, rate_ref, gain, full, narrow, sums, at_sum):
@@ -891,7 +965,6 @@
     slope_part(0)
     reduced.finish(*((1,) if last else BOTH))
     if not last:
-        line.middle()
         before.middle(1)
     plane.start(*((1,) if last else BOTH))
     slope_part(ff // 2)
@@ -910,10 +983,11 @@
     for part in BOTH:
         expand_part(part, core, k.e_mine)
     if not last:
-        line.spread()
         before.finish()
         late = LineSum(k, "y_", k.x_total)
         late.start()
+        line.settle()
+        line.give(k, k.o_z)
     else:
         plane.middle(0)
     got_up.wait()
@@ -943,8 +1017,6 @@
         outward.wait()
         k.save(k.regrouped, k.o_out)
     else:
-        line.finish()
-        k.save(k.z_whole, k.o_z)
         late.settle()
         late.give(k, k.o_y)
     plane.finish()
@@ -952,7 +1024,7 @@
     k.done()
 
 
-def pooled_back(k, layer, rows, width):
+def pooled_back(k, layer, rows, width, last):
     core = lax.axis_index("seq") % 2
     sibling, across, up, line_peers, _ = axis_peers()
     pool = rows // 4
@@ -961,15 +1033,14 @@
     got = k.load_all(["dy2"])
     got_mix = k.load(k.w_mix2.at[layer], k.v_mix2)
     got_small = k.load(k.small_in, k.small)
-    late = LineSum(k, "y_", k.y_in) if hasattr(k, "y_in") else None
-    if late:
-        got_late = late.take()
+    late = [] if last else [LineSum(k, "y_", k.y_in), LineSum(k, "w_", k.w_in)]
+    got_late = [copy for each in late for copy in each.take()]
     greet([sibling, across, up] + line_peers)
     plane, line = PlaneSum(k, "x_", k.x_in), LineSum(k, "z_", k.z_in)
-    if late:
-        for copy in got_late:
-            copy.wait()
-        late.gather()
+    for copy in got_late:
+        copy.wait()
+    for each in late:
+        each.gather()
     plane.start()
     line.start()
     got.update(k.load_all("q2 pk".split()))
@@ -1011,7 +1082,7 @@
     turn(k.v_b, k.b_t)
     got["kv2"].wait()
     for c in range(2 * width // 128):
-        k.kvf[c] = k.v_kv2[:, pl.ds(c * 128, 128)].astype(F32)
+        k.kvf[c, :rows] = k.v_kv2[:, pl.ds(c * 128, 128)].astype(F32)
     got_small.wait()
     rim.wait()
     k.total[pl.ds(0, pool)] = (
@@ -1038,12 +1109,16 @@
         k.kvf[c, rows_at[1]] = own * taps[3]
         k.kvf[c, rows_at[2]] = own * taps[4] + after * taps[0]
         k.kvf[c, rows_at[3]] = after * taps[1]
-        k.dqkv[:, pl.ds(width + c * 128, 128)] = k.kvf[c].astype(BF16)
+        k.dqkv[:, pl.ds(width + c * 128, 128)] = k.kvf[c, :rows].astype(BF16)
     turn(k.dqkv, k.dqkv_t)
     got["x1"].wait()
-    if late:
-        late.spread()
-    line.middle()
+    for each in late:
+        each.spread()
+    line.settle()
+    if last:
+        line.gather()
+    else:
+        line.give(k, k.o_z)
     plane.middle()
     summed = CoreSum(k, "p_")
     middle = width // 2
@@ -1095,16 +1170,19 @@
     k.save(k.v_mid, k.o_low)
     k.save(k.dn, k.o_dy1)
     save_sums(k, 2, k.tap_sums)
-    line.spread()
+    if last:
+        line.spread()
     plane.finish()
     k.save(k.x_total, k.o_x)
     summed.finish()
     k.save(k.p_mine, k.o_p)
-    if late:
-        late.finish()
-        k.save(k.y_whole, k.o_y)
-    line.finish()
-    k.save(k.z_whole, k.o_z)
+    if last:
+        line.finish()
+        k.save(k.z_whole, k.o_z)
+    else:
+        for each, target in zip(late, (k.o_y, k.o_w)):
+            each.finish()
+            k.save(each.whole, target)
     k.done()
 
 
@@ -1127,6 +1205,8 @@
     if final:
         small = SmallSum(k)
         small.load()
+        early = LineSum(k, "r_", k.r_in)
+        got_early = early.take()
     for i in range(blocks):
         k.lbias[i] = local_bias_turned(i, blocks, core == 0, core == 1, 128, half)
     got["dy1"].wait()
@@ -1193,11 +1273,11 @@
             k.v_low[:, i : i + 256] += dot_nt(k.dqkv[...], k.v_local[i : i + 256])
 
     if not final:
+        line.middle()
+        plane.middle()
         for part in BOTH:
             grad_part(part, 1 - core, k.l_send)
             summed.start(part)
-        line.middle()
-        plane.middle()
         for part in BOTH:
             grad_part(part, core, k.l_mine)
         residual()
@@ -1217,32 +1297,43 @@
         k.narrow[i // 128] = k.v_low[i : i + 128].astype(BF16)
     outward = Regroup(k.loads, k.links, k.narrow, k.regrouped, False)
     outward.start()
-    line.middle()
     plane.middle()
+    line.settle()
     for part in BOTH:
         grad_part(part, 1 - core, k.l_send)
         summed.start(part)
     small.step()
-    last_plane, last_line = PlaneSum(k, "l_", k.l_mine), LineSum(k, "f_", k.l_total)
+    last_plane, last_line = PlaneSum(k, "l_", k.l_mine), RelaySum(k, "f_", k.l_total)
     for part in BOTH:
         grad_part(part, core, k.l_mine)
     for part in BOTH:
         summed.finish(part)
         last_plane.start(part)
     plane.finish()
-    before = LineSum(k, "p_", k.x_total)
+    before = RelaySum(k, "p_", k.x_total)
     before.start()
     small.step()
-    line.spread()
     last_plane.middle(0)
+    for copy in got_early:
+        copy.wait()
     last_plane.middle(1)
-    line.finish()
-    k.save(k.z_whole, k.o_z)
-    before.middle()
+    before.relay(0)
+    before.relay(1)
+    line.gather()
+    early.gather()
     for part in BOTH:
         last_plane.finish(part)
         last_line.start(part)
+    before.settle()
+    line.spread()
+    early.spread()
+    last_line.relay(0)
+    before.gather()
+    last_line.relay(1)
     small.finish()
+    for each, target in ((line, k.o_z), (early, k.o_r)):
+        each.finish()
+        k.save(each.whole, target)
     before.spread()
     outward.wait()
     k.save(k.regrouped, k.o_dx)
@@ -1260,35 +1351,46 @@
 class SmallSum:
     def __init__(self, k):
         self.k = k
-        sibling, across, up, line, _ = axis_peers()
-        self.order = [[sibling], [across], [up], line]
-        self.at, self.slot = 0, 0
+        sibling, across, up, self.line, self.along = axis_peers()
+        self.order = [sibling, across, up]
+        self.at = 0
 
     def load(self):
         k = self.k
         self.copies = []
-        for i in range(k.s_sum.shape[0]):
-            for source, first, last in ((k.s_feed[i], 0, 8), (k.s_pool[i], 8, 24)):
-                self.copies.append(k.load(source, k.s_sum.at[i, first:last]))
+        for i, (feed, pooled) in enumerate(zip(k.s_feed, k.s_pool)):
+            self.copies.append(k.load(feed, k.s_sum.at[24 * i : 24 * i + 8]))
+            self.copies.append(k.load(pooled, k.s_sum.at[24 * i + 8 : 24 * i + 24]))
+
+    def window(self, z):
+        return pl.ds(pl.multiple_of(3 * z // 2 * 128, 128), 256)
 
     def step(self):
         k = self.k
         for copy in self.copies:
             copy.wait()
         if self.at > 0:
-            for _ in self.copies:
-                k.s_sum[...] += k.s_got[self.slot]
-                self.slot += 1
+            k.s_sum[...] += k.s_got[self.at - 1].astype(F32)
+        k.s_out[...] = k.s_sum[...].astype(BF16)
         if self.at < len(self.order):
+            self.copies = [k.links.start(k.s_out, k.s_got.at[self.at], self.order[self.at])]
+        else:
             self.copies = [
-                k.links.start(k.s_sum, k.s_got.at[self.slot + i], device)
-                for i, device in enumerate(self.order[self.at])
+                k.links.start(k.s_out.at[:, self.window(z)], k.s_line.at[i], device)
+                for i, (z, device) in enumerate(zip(self.along, self.line))
             ]
         self.at += 1
 
     def finish(self):
-        self.step()
-        self.k.save(self.k.s_sum, self.k.o_small)
+        k = self.k
+        for copy in self.copies:
+            copy.wait()
+        mine = self.window(lax.axis_index("seq") // 2)
+        total = k.s_sum[:, mine]
+        for i in range(3):
+            total = total + k.s_line[i].astype(F32)
+        k.s_sum[:, mine] = total
+        k.save(k.s_sum, k.o_small)
 
 
 def save_sums(k, count, taps=None):
@@ -1347,7 +1449,7 @@
         s.add(regrouped=vmem(by_doc))
     else:
         args.update(x_in=(x_in, ANY), z_in=(z_in, ANY))
-        outs.update(o_y=((2, 2) + block, BF16), o_z=(whole_shape(block), BF16))
+        outs.update(o_y=((2, 2) + block, BF16), o_z=((2, 2) + block, BF16))
         s.plane("x_", block)
         s.line("y_", block)
         s.line("z_", block)
@@ -1362,7 +1464,9 @@
     )
 
 
-def pooled_back_call(layer, mid, dy2, small, pbias, kept, w_mix2, w_pooled, x_in, z_in, y_in):
+def pooled_back_call(
+    layer, last, mid, dy2, small, pbias, kept, w_mix2, w_pooled, x_in, z_in, y_in, w_in
+):
     rows, width = mid.shape
     pool = rows // 4
     block = block_of(width)
@@ -1374,25 +1478,26 @@
     s.bring(args, x1=kept.o_x1, xh1=kept.o_xh1, r1=kept.o_r1, pbias=pbias)
     outs = dict(o_low=(full, F32), o_dy1=(full, BF16), o_sums=((16, width), F32))
     outs.update(o_p=(group_shape(block), BF16), o_x=(total_shape(block), BF16))
-    outs.update(o_z=(whole_shape(block), BF16))
+    outs.update(o_z=(whole_shape(block) if last else (2, 2) + block, BF16))
     s.add(small=vmem(small.shape, F32), v_mix2=vmem(w_mix2.shape[1:]))
     s.add(v_pooled=vmem(w_pooled.shape[1:]), sums=vmem((2, 8, width), F32))
     s.add(row_sums=vmem((16, width), F32), tap_sums=vmem((2, 40, width), F32), do=wide, dn=wide)
     rim, turned = vmem((pool + 16, 2 * width)), vmem((width, rows))
     s.add(dkv=vmem((2 * pool, 2 * width), F32), rim_out=rim, rim_got=rim)
-    s.add(total=vmem((pool + 8, 2 * width), F32), kvf=vmem((2 * width // 128, rows, 128), F32))
+    s.add(total=vmem((pool + 8, 2 * width), F32), kvf=vmem((2 * width // 128, rows + 8, 128), F32))
     s.add(dqkv=vmem((rows, 3 * width)), dqkv_t=vmem((3 * width, rows)), b_t=turned)
     s.add(mixed=vmem((width // 2, width // 2), F32))
     s.core("p_", block)
     s.plane("x_", block)
     s.line("z_", block)
-    if y_in is not None:
-        args.update(y_in=(y_in, ANY))
-        outs.update(o_y=(whole_shape(block), BF16))
-        s.add(y_whole=vmem(whole_shape(block)))
+    if not last:
+        args.update(y_in=(y_in, ANY), w_in=(w_in, ANY))
+        whole = whole_shape(block)
+        outs.update(o_y=(whole, BF16), o_w=(whole, BF16))
+        s.add(y_whole=vmem(whole), w_whole=vmem(whole))
     s.sems(40, 16, 48)
     return run_kernel(
-        lambda k: pooled_back(k, layer, rows, width),
+        lambda k: pooled_back(k, layer, rows, width, last),
         "pooled_back_%d" % layer,
         4 + layer,
         args,
@@ -1401,7 +1506,7 @@
     )
 
 
-def local_back_call(layer, final, low, dy1, kept, w_mix, w_local, x_in, z_in, sums):
+def local_back_call(layer, final, low, dy1, kept, w_mix, w_local, x_in, z_in, r_in, sums):
     rows, width = low.shape
     half = LOCAL_WIN // 2
     block = block_of(width)
@@ -1409,12 +1514,14 @@
     args = dict(w_mix=(w_mix, ANY), w_local=(w_local, ANY), x_in=(x_in, ANY), z_in=(z_in, ANY))
     s.bring(args, low=low, dy1=dy1, a=kept.o_a, q=kept.o_q, kv=kept.o_kv, x=kept.o_x)
     outs = dict(o_z=(whole_shape(block), BF16))
-    by_doc, total = (4, rows // 4, width), (len(sums), 24, width)
+    by_doc, total = (4, rows // 4, width), (len(sums) * 24, width)
     if final:
         whole = (whole_shape(block), BF16)
         for i, (feed, pooled) in enumerate(sums):
             args["s_feed%d" % i], args["s_pool%d" % i] = (feed, ANY), (pooled, ANY)
-        outs.update(o_dx=(by_doc, BF16), o_p=whole, o_f=whole, o_small=(total, F32))
+        args.update(r_in=(r_in, ANY))
+        outs.update(o_dx=(by_doc, BF16), o_p=whole, o_f=whole, o_r=whole, o_small=(total, F32))
+        s.add(r_whole=vmem(whole_shape(block)))
     else:
         outs.update(o_dx=((rows, width), F32), o_l=(group_shape(block), BF16))
         outs.update(o_x=(total_shape(block), BF16))
@@ -1429,11 +1536,12 @@
     s.line("z_", block)
     if final:
         s.add(narrow=vmem(by_doc), regrouped=vmem(by_doc))
-        s.add(s_sum=vmem(total, F32), s_got=vmem((6,) + total, F32))
+        s.add(s_sum=vmem(total, F32), s_out=vmem(total), s_got=vmem((3,) + total))
+        s.add(s_line=vmem((3, len(sums) * 24, 256)))
         s.plane("l_", block)
         s.line("p_", block)
         s.line("f_", block)
-    s.sems(48, 16, 72)
+    s.sems(48, 16, 96)
 
     def body(k):
         if final:
@@ -1489,10 +1597,9 @@
         )
         if last:
             outputs = fed.o_out
-        else:
-            pooled_sums[layer + 1] = fed.o_z
         pooled = pooled_back_call(
             layer,
+            last,
             fed.o_mid,
             fed.o_dy2,
             small,
@@ -1503,10 +1610,10 @@
             fed.o_e,
             fed.o_r,
             None if last else fed.o_y,
-        )
-        reduced[layer] = pooled.o_z
+            None if last else fed.o_z,
+        )
         if not last:
-            local_sums[layer + 1] = pooled.o_y
+            local_sums[layer + 1], pooled_sums[layer + 1] = pooled.o_y, pooled.o_w
         sums.insert(0, (fed.o_sums, pooled.o_sums))
         local = local_back_call(
             layer,
@@ -1518,8 +1625,10 @@
             local_proj,
             pooled.o_p,
             pooled.o_x,
+            None if last else pooled.o_z,
             sums,
         )
+        reduced[layer] = pooled.o_z if last else local.o_r
         expanded[layer] = local.o_z
         if layer > 0:
             grad, x_in, z_in = local.o_dx, local.o_l, local.o_x
@@ -1566,11 +1675,11 @@
         put(layer, k.v_mix2, k.o_mix2, pooled[3 * part :])
     got_small.wait()
     small = k.v_small_sum[...]
-    mine = jnp.zeros(small.shape[:2] + (part,), F32)
+    mine = jnp.zeros((small.shape[0], part), F32)
     for i in range(8):
-        mine = jnp.where(me == i, small[:, :, i * part : (i + 1) * part], mine)
+        mine = jnp.where(me == i, small[:, i * part : (i + 1) * part], mine)
     for layer in range(layers):
-        rows = mine[layer]
+        rows = mine[24 * layer : 24 * layer + 24]
         for i, (gain, shift) in enumerate(((8, 9), (2, 3), (0, 1))):
             k.v_gain[i, layer : layer + 1] = rows[gain : gain + 1]
             k.v_shift[i, layer : layer + 1] = rows[shift : shift + 1]

time: 354 us -> 341 us (0.963); the launches traced: 349 us -> 339 us
  Pallas kernels: 345 us -> 335 us
    pallas_call x9, Pallas kernels: 345 us -> 335 us  [run_kernel(): pl.pallas_call(kernel, out_shape=[jax.ShapeDtypeStruct(shape, kind) for s...]
where the time goes in v2:
time: 341 us; the launch traced here: 339 us
  Pallas kernels  335 us (98%)
    pallas_call x9, Pallas kernels, run_kernel(): pl.pallas_call(kernel, out_shape=[jax.ShapeDtypeStruct(shape, kind) for s...  335 us

profile of v2, /device:TPU:0, one launch (start us, length us, event | category | flops | bytes accessed | tf_op | source)
XLA Modules:
  0.0 339.4 jit_solution(8645054740140832223)
XLA Ops:
  0.6 0.7 copy.29
  1.4 0.7 copy.30
  2.1 0.9 copy.28
  3.0 0.7 pad_maximum_fusion.refs_1_.refs_0_
  3.7 45.9 %forward_0.1 = (bf16[4,128,768]{2,1,0:T(8,128)(2,1)}, bf16[512,768]{1,0:T(8,128)(2,1)}, bf16[640,1536]{1,0:T(8,128)(2,1)}, bf16[512,768]{1,0:T(8,128)(2,1)}, bf1...) custom-call(bf16[4,128,768]{2,1,0:T(8,128)(2,1)} %refs_0_.3, ...), custom_call_target="tpu_custom_call" | custom-call | tf_op jit(solution)/shard_map/forward_0/pallas_call | solution.py:310
  49.6 37.9 %forward_1.1 = (bf16[512,768]{1,0:T(8,128)(2,1)}, bf16[512,768]{1,0:T(8,128)(2,1)}, bf16[640,1536]{1,0:T(8,128)(2,1)}, bf16[512,768]{1,0:T(8,128)(2,1)}, bf16[51...) custom-call(f32[512,768]{1,0:T(8,128)} %get-tuple-element.103.refs_0, ...), custom_call_target="tpu_custom_call" | custom-call | tf_op jit(solution)/shard_map/forward_1/pallas_call | solution.py:310
  87.5 38.0 %feed_back_1.1 = (f32[512,768]{1,0:T(8,128)}, bf16[512,768]{1,0:T(8,128)(2,1)}, f32[8,768]{1,0:T(8,128)}, bf16[2,4,2,48,384]{4,3,2,1,0:T(8,128)(2,1)}, bf16[2,4,...) custom-call(f32[2,16,768]{2,1,0:T(8,128)} %pad_maximum_fusion.refs_1_.refs_0_, ...), custom_call_target="tpu_custom_call" | custom-call | tf_op jit(solution)/shard_map/feed_back_1/pallas_call | solution.py:310
  125.5 29.2 %pooled_back_1.1 = (f32[512,768]{1,0:T(8,128)}, bf16[512,768]{1,0:T(8,128)(2,1)}, f32[16,768]{1,0:T(8,128)}, bf16[2,4,2,2,2,48,384]{6,5,4,3,2,1,0:T(8,128)(2,1)}...) custom-call(f32[2,16,768]{2,1,0:T(8,128)} %pad_maximum_fusion.refs_1_.refs_0_, ...), custom_call_target="tpu_custom_call" | custom-call | tf_op jit(solution)/shard_map/pooled_back_1/pallas_call | solution.py:310
  154.7 29.9 %local_back_1.1 = (bf16[2,2,2,2,48,384]{5,4,3,2,1,0:T(8,128)(2,1)}, f32[512,768]{1,0:T(8,128)}, bf16[2,4,2,2,2,48,384]{6,5,4,3,2,1,0:T(8,128)(2,1)}, bf16[2,4,2,48,384]{4,3,2,1,0:T(8,128)(2,1)}) custom-call(bf16[2,768,768]{2,1,0:T(8,128)(2,1)} %refs_0_.5, bf16[2,768,2304]{2,1,0:T(8,128)(2,1)} %refs_1_.11, ...), custom_call_target="tpu_custom_call" | custom-call | tf_op jit(solution)/shard_map/local_back_1/pallas_call | solution.py:310
  184.6 43.3 %feed_back_0.1 = (f32[512,768]{1,0:T(8,128)}, bf16[512,768]{1,0:T(8,128)(2,1)}, f32[8,768]{1,0:T(8,128)}, bf16[2,4,2,48,384]{4,3,2,1,0:T(8,128)(2,1)}, bf16[2,4,...) custom-call(f32[2,16,768]{2,1,0:T(8,128)} %pad_maximum_fusion.refs_1_.refs_0_, ...), custom_call_target="tpu_custom_call" | custom-call | tf_op jit(solution)/shard_map/feed_back_0/pallas_call | solution.py:310
  227.9 34.2 %pooled_back_0.1 = (f32[512,768]{1,0:T(8,128)}, bf16[512,768]{1,0:T(8,128)(2,1)}, f32[16,768]{1,0:T(8,128)}, bf16[2,4,2,2,2,48,384]{6,5,4,3,2,1,0:T(8,128)(2,1)}...) custom-call(f32[2,16,768]{2,1,0:T(8,128)} %pad_maximum_fusion.refs_1, ...), custom_call_target="tpu_custom_call" | custom-call | tf_op jit(solution)/shard_map/pooled_back_0/pallas_call | solution.py:310
  262.1 69.8 %local_back_0.1 = (bf16[2,2,2,2,48,384]{5,4,3,2,1,0:T(8,128)(2,1)}, bf16[4,128,768]{2,1,0:T(8,128)(2,1)}, bf16[2,2,2,2,48,384]{5,4,3,2,1,0:T(8,128)(2,1)}, bf16[...) custom-call(bf16[2,768,768]{2,1,0:T(8,128)(2,1)} %refs_0_.5, ...), custom_call_target="tpu_custom_call" | custom-call | tf_op jit(solution)/shard_map/local_back_0/pallas_call | solution.py:310
  331.9 7.2 %finish.1 = (bf16[4,128,768]{2,1,0:T(8,128)(2,1)}, f32[4,128,768]{2,1,0:T(8,128)}, f32[2,288,768]{2,1,0:T(8,128)}, f32[2,96,768]{2,1,0:T(8,128)}, f32[2,96,768]{...) custom-call(bf16[4,128,768]{2,1,0:T(8,128)(2,1)} %get-tuple-element., ...), custom_call_target="tpu_custom_call" | custom-call | tf_op jit(solution)/shard_map/finish/pallas_call | solution.py:310
  (1 shorter events, 0.0 us)

commit v3 on v2

--- a/solution.py
+++ b/solution.py
@@ -190,12 +190,11 @@
     return stacked[:rows] * low + stacked[rows:] * high
 
 
-def attend_blocks(queries, key_rows, value_rows, bias):
+def attend_blocks(queries, key_rows, value_rows, biases):
     low, high = split_masks(2 * HD)
-    wide_bias = jnp.concatenate([bias, bias], 0)
     scores = [
-        dot_nt(by_head(query, low, high, HD**-0.5), key) + wide_bias
-        for query, key in zip(queries, key_rows)
+        dot_nt(by_head(query, low, high, HD**-0.5), key) + jnp.concatenate([bias, bias], 0)
+        for query, key, bias in zip(queries, key_rows, biases)
     ]
     soft = []
     for score in scores:
@@ -417,17 +416,22 @@
     k.save(k.kv, k.o_kv)
 
     def attend_local(i):
-        here, seen = aligned(i, 128), pl.ds(pl.multiple_of(i * 128, 128), 128 + 2 * half)
+        items = [
+            (2 * i + j, lanes, values)
+            for j in range(2)
+            for lanes, values in zip(lanes_of, values_of)
+        ]
+        seen = [pl.ds(pl.multiple_of(at * 128, 128), 128 + 2 * half) for at, _, _ in items]
         mixed = attend_blocks(
-            [k.q[here, lanes] for lanes in lanes_of],
-            [k.kv[seen, lanes] for lanes in lanes_of],
-            [k.kv[seen, lanes] for lanes in values_of],
-            k.lbias[i],
-        )
-        for lanes, part in zip(lanes_of, mixed):
-            k.a[here, lanes] = part
-
-    loop(blocks, attend_local)
+            [k.q[aligned(at, 128), lanes] for at, lanes, _ in items],
+            [k.kv[keys, lanes] for keys, (_, lanes, _) in zip(seen, items)],
+            [k.kv[keys, values] for keys, (_, _, values) in zip(seen, items)],
+            [k.lbias[at] for at, _, _ in items],
+        )
+        for (at, lanes, _), part in zip(items, mixed):
+            k.a[aligned(at, 128), lanes] = part
+
+    loop(blocks // 2, attend_local)
     k.save(k.a, k.o_a)
     got += [weight(k.w_mix2, k.wm2), weight(k.w_up, k.wu), weight(k.w_down, k.wd)]
     if first:
@@ -493,17 +497,21 @@
     k.save(k.pk, k.o_pk)
 
     def attend_pooled(i):
-        here = aligned(i, 128)
+        items = [
+            (aligned(2 * i + j, 128), lanes, values)
+            for j in range(2)
+            for lanes, values in zip(lanes_of, values_of)
+        ]
         mixed = attend_blocks(
-            [k.q2[here, lanes] for lanes in lanes_of],
-            [k.pk[:, lanes] for lanes in lanes_of],
-            [k.pk[:, lanes] for lanes in values_of],
-            k.pbias[here],
-        )
-        for lanes, part in zip(lanes_of, mixed):
+            [k.q2[here, lanes] for here, lanes, _ in items],
+            [k.pk[:, lanes] for _, lanes, _ in items],
+            [k.pk[:, values] for _, _, values in items],
+            [k.pbias[here] for here, _, _ in items],
+        )
+        for (here, lanes, _), part in zip(items, mixed):
             k.b[here, lanes] = part
 
-    loop(blocks, attend_pooled)
+    loop(blocks // 2, attend_pooled)
     k.save(k.b, k.o_b)
     got[3].wait()
     mix_norm(1, k.b, k.wm2, k.x1f, k.xh2, k.rt2, k.x1f, k.x2)
@@ -941,26 +949,28 @@
                 dot_nt(k.dn[...], k.v_down[i : i + 512]) * k.v_gp[:, i : i + 512].astype(F32)
             ).astype(BF16)
 
+    plane = PlaneSum(k, "r_", k.r_mine)
     reduce_part(0, 1 - core, k.r_send)
     if last:
         greet_regroup([sibling, across, up] + line_peers)
     reduced.start(0)
+    if last:
+        reduce_part(0, core, k.r_mine)
     reduce_part(1, 1 - core, k.r_send)
     reduced.start(1)
     got.update(k.load_all("x2 xh2 r2".split()))
     got_up = k.load(k.w_up.at[layer], k.v_up)
-    reduce_part(0, core, k.r_mine)
-    reduce_part(1, core, k.r_mine)
-    if last:
-        outward = Regroup(k.loads, k.links, k.x3, k.regrouped, False)
-        outward.start()
-    got["gp"].wait()
-    got_down.wait()
-    plane = PlaneSum(k, "r_", k.r_mine)
     if last:
         reduced.finish(0)
         plane.start(0)
+        outward = Regroup(k.loads, k.links, k.x3, k.regrouped, False)
+        outward.start()
     else:
+        reduce_part(0, core, k.r_mine)
+    reduce_part(1, core, k.r_mine)
+    got["gp"].wait()
+    got_down.wait()
+    if not last:
         before.middle(0)
     slope_part(0)
     reduced.finish(*((1,) if last else BOTH))
@@ -1194,6 +1204,7 @@
     shard = width // 8
     got = k.load_all(["dy1"])
     got_mix = k.load(k.w_mix.at[layer], k.v_mix)
+    got.update(k.load_all("q kv".split()))
     if final:
         greet_regroup([sibling, across, up] + line_peers)
     else:
@@ -1201,7 +1212,6 @@
     plane, line = PlaneSum(k, "x_", k.x_in), LineSum(k, "z_", k.z_in)
     plane.start()
     line.start()
-    got.update(k.load_all("q kv".split()))
     if final:
         small = SmallSum(k)
         small.load()

time: 341 us -> 342 us (level)
  no operation moved by 1% of the time
where the time goes in v3:
time: 342 us; the launch traced here: 341 us
  Pallas kernels  337 us (99%)
    pallas_call x9, Pallas kernels, run_kernel(): pl.pallas_call(kernel, out_shape=[jax.ShapeDtypeStruct(shape, kind) for s...  337 us

profile of v3, /device:TPU:0, one launch (start us, length us, event | category | flops | bytes accessed | tf_op | source)
XLA Modules:
  0.0 341.0 jit_solution(14048947208561077236)
XLA Ops:
  0.6 0.7 copy.29
  1.4 0.7 copy.30
  2.1 0.9 copy.28
  3.0 0.7 pad_maximum_fusion.refs_1_.refs_0_
  3.7 45.4 %forward_0.1 = (bf16[4,128,768]{2,1,0:T(8,128)(2,1)}, bf16[512,768]{1,0:T(8,128)(2,1)}, bf16[640,1536]{1,0:T(8,128)(2,1)}, bf16[512,768]{1,0:T(8,128)(2,1)}, bf1...) custom-call(bf16[4,128,768]{2,1,0:T(8,128)(2,1)} %refs_0_.3, ...), custom_call_target="tpu_custom_call" | custom-call | tf_op jit(solution)/shard_map/forward_0/pallas_call | solution.py:309
  49.1 39.8 %forward_1.1 = (bf16[512,768]{1,0:T(8,128)(2,1)}, bf16[512,768]{1,0:T(8,128)(2,1)}, bf16[640,1536]{1,0:T(8,128)(2,1)}, bf16[512,768]{1,0:T(8,128)(2,1)}, bf16[51...) custom-call(f32[512,768]{1,0:T(8,128)} %get-tuple-element.103.refs_0, ...), custom_call_target="tpu_custom_call" | custom-call | tf_op jit(solution)/shard_map/forward_1/pallas_call | solution.py:309
  88.9 37.9 %feed_back_1.1 = (f32[512,768]{1,0:T(8,128)}, bf16[512,768]{1,0:T(8,128)(2,1)}, f32[8,768]{1,0:T(8,128)}, bf16[2,4,2,48,384]{4,3,2,1,0:T(8,128)(2,1)}, bf16[2,4,...) custom-call(f32[2,16,768]{2,1,0:T(8,128)} %pad_maximum_fusion.refs_1_.refs_0_, ...), custom_call_target="tpu_custom_call" | custom-call | tf_op jit(solution)/shard_map/feed_back_1/pallas_call | solution.py:309
  126.9 29.4 %pooled_back_1.1 = (f32[512,768]{1,0:T(8,128)}, bf16[512,768]{1,0:T(8,128)(2,1)}, f32[16,768]{1,0:T(8,128)}, bf16[2,4,2,2,2,48,384]{6,5,4,3,2,1,0:T(8,128)(2,1)}...) custom-call(f32[2,16,768]{2,1,0:T(8,128)} %pad_maximum_fusion.refs_1_.refs_0_, ...), custom_call_target="tpu_custom_call" | custom-call | tf_op jit(solution)/shard_map/pooled_back_1/pallas_call | solution.py:309
  156.2 30.0 %local_back_1.1 = (bf16[2,2,2,2,48,384]{5,4,3,2,1,0:T(8,128)(2,1)}, f32[512,768]{1,0:T(8,128)}, bf16[2,4,2,2,2,48,384]{6,5,4,3,2,1,0:T(8,128)(2,1)}, bf16[2,4,2,48,384]{4,3,2,1,0:T(8,128)(2,1)}) custom-call(bf16[2,768,768]{2,1,0:T(8,128)(2,1)} %refs_0_.5, bf16[2,768,2304]{2,1,0:T(8,128)(2,1)} %refs_1_.11, ...), custom_call_target="tpu_custom_call" | custom-call | tf_op jit(solution)/shard_map/local_back_1/pallas_call | solution.py:309
  186.2 43.7 %feed_back_0.1 = (f32[512,768]{1,0:T(8,128)}, bf16[512,768]{1,0:T(8,128)(2,1)}, f32[8,768]{1,0:T(8,128)}, bf16[2,4,2,48,384]{4,3,2,1,0:T(8,128)(2,1)}, bf16[2,4,...) custom-call(f32[2,16,768]{2,1,0:T(8,128)} %pad_maximum_fusion.refs_1_.refs_0_, ...), custom_call_target="tpu_custom_call" | custom-call | tf_op jit(solution)/shard_map/feed_back_0/pallas_call | solution.py:309
  229.9 34.6 %pooled_back_0.1 = (f32[512,768]{1,0:T(8,128)}, bf16[512,768]{1,0:T(8,128)(2,1)}, f32[16,768]{1,0:T(8,128)}, bf16[2,4,2,2,2,48,384]{6,5,4,3,2,1,0:T(8,128)(2,1)}...) custom-call(f32[2,16,768]{2,1,0:T(8,128)} %pad_maximum_fusion.refs_1, ...), custom_call_target="tpu_custom_call" | custom-call | tf_op jit(solution)/shard_map/pooled_back_0/pallas_call | solution.py:309
  264.5 69.0 %local_back_0.1 = (bf16[2,2,2,2,48,384]{5,4,3,2,1,0:T(8,128)(2,1)}, bf16[4,128,768]{2,1,0:T(8,128)(2,1)}, bf16[2,2,2,2,48,384]{5,4,3,2,1,0:T(8,128)(2,1)}, bf16[...) custom-call(bf16[2,768,768]{2,1,0:T(8,128)(2,1)} %refs_0_.5, ...), custom_call_target="tpu_custom_call" | custom-call | tf_op jit(solution)/shard_map/local_back_0/pallas_call | solution.py:309
  333.5 7.2 %finish.1 = (bf16[4,128,768]{2,1,0:T(8,128)(2,1)}, f32[4,128,768]{2,1,0:T(8,128)}, f32[2,288,768]{2,1,0:T(8,128)}, f32[2,96,768]{2,1,0:T(8,128)}, f32[2,96,768]{...) custom-call(bf16[4,128,768]{2,1,0:T(8,128)(2,1)} %get-tuple-element., ...), custom_call_target="tpu_custom_call" | custom-call | tf_op jit(solution)/shard_map/finish/pallas_call | solution.py:309
  (1 shorter events, 0.0 us)
